TPU v7x, 256 devices: a whole 4x4x8 slice. The times are simulated.
256 devices in a mesh: dom: 16 (over z, core), st: 16 (over x, y).
Axes of the slice: x: 4, y: 4, z: 8, core: 2. Of those that a mesh axis runs over, the one named last changes fastest.
Arguments:
- inv_sqrt_blocks: bfloat16 [1024, 8, 128, 128], P('dom'), may hold values from -0.1875 to 0.1875
- waves: bfloat16 [512, 131072], P('st', 'dom'), may hold values from -0.59765625 to 0.59765625
- occupation: float32 [512], P('st'), may hold values from 0 to 2
- block_ref: int32 [1024, 8], P('dom'), may hold values from 0 to 127, as said below
- row_count: int32 [1024], P('dom'), may hold values from 2 to 8
- send_list: int32 [16, 4, 16], P('dom'), may hold values from 0 to 63
Outputs:
- density: float32 [1024, 8, 128, 128], P('dom', None, 'st')
Inputs may be any that keep to these rules, and one draw needn't show every extreme that they name: `block_ref`: slot 0 names the row's own block, slot 1 another block of the same domain, slots 2 and on codes 64 and above of blocks received from neighbouring domains.
All inputs are finite; a program needn't handle non-finite values.
Results may differ from a plain program's by a relative error of at most 0.0037.
Values may be sent and summed in bfloat16 or wider, within the bound.
No kernel may reach another device: no remote copies, remote signals or barrier semaphores. Data moves between devices by JAX's collectives and lax.ppermute only.
A program may use at most 192 MiB of HBM per device.

v0:
```python
import jax
import jax.numpy as jnp
from jax import lax
from jax.sharding import PartitionSpec as P

neighbour_offsets = (-2, -1, 1, 2)


def passed_along(value, axis, by):
    count = lax.axis_size(axis)
    return lax.ppermute(value, axis, [(i, (i + by) % count) for i in range(count)])


def body(inv_sqrt_blocks, waves, occupation, block_ref, row_count, send_list):
    blocks_here, neighbours, block_size, _ = inv_sqrt_blocks.shape
    states_here = waves.shape[0]
    live = jnp.arange(neighbours, dtype=jnp.int32)[None, :] < row_count[:, None]
    own_blocks = waves.reshape(states_here, blocks_here, block_size)
    pieces = []
    for slot, offset in enumerate(neighbour_offsets):
        outgoing = own_blocks[:, send_list[0, slot]]
        pieces.append(passed_along(outgoing, "dom", offset))
    table = jnp.concatenate([own_blocks] + pieces, axis=1)
    operand = table[:, block_ref] * live[None, :, :, None].astype(jnp.bfloat16)
    coef = jnp.einsum(
        "sikc,ikrc->sir", operand, inv_sqrt_blocks, preferred_element_type=jnp.float32
    ).astype(jnp.bfloat16)
    coef_pieces = []
    for slot, offset in enumerate(neighbour_offsets):
        coef_out = coef[:, send_list[0, slot]]
        coef_pieces.append(passed_along(coef_out, "dom", offset))
    coef_table = jnp.concatenate([coef] + coef_pieces, axis=1)
    weighted = (occupation[:, None, None] * coef).astype(jnp.bfloat16)
    alive = live[:, :, None, None].astype(jnp.float32)
    partner = coef_table[:, block_ref]
    partial_terms = (
        jnp.einsum("sir,sikc->ikrc", weighted, partner, preferred_element_type=jnp.float32) * alive
    )
    density = lax.psum_scatter(partial_terms, "st", scatter_dimension=2, tiled=True)
    return density


def solution(mesh):
    in_specs = (
        P("dom", None, None, None),
        P("st", "dom"),
        P("st"),
        P("dom", None),
        P("dom"),
        P("dom", None, None),
    )
    out_specs = P("dom", None, "st", None)
    return jax.shard_map(body, mesh=mesh, in_specs=in_specs, out_specs=out_specs, check_vma=False)
```

profile of v0, /device:TPU:24, one launch (start us, length us, event | category | flops | bytes accessed | tf_op | source)
XLA Modules:
  0.0 308.7 jit_solution(13898949734821389876)
XLA Ops:
  6.5 0.8 fusion.21
  7.7 0.6 gather_fusion
  8.3 5.9 %collective-permute-start = (bf16[32,16,128]{2,0,1:T(8,128)(2,1)S(1)}, bf16[32,16,128]{2,0,1:T(8,128)(2,1)S(1)}, u32[]{:S(2)}, u32[]{:S(2)}) collective-permute-start(bf16[32,16,128]{2,0,1:T(8,128)(2,1)S(1)} %bitcast.69), channel_id=1, source_target_pairs={{0,224},{16,240},{32,0},{48,16},{64,32},{80,48},{96,64},{112,80},{... | collective-permute-start | bytes 393224 | tf_op jit(solution)/shard_map/ppermute | solution.py:11
  14.3 0.6 gather_fusion.3
  14.9 0.6 gather_fusion.1
  15.5 2.1 collective-permute-start.1
  18.3 0.7 fusion.17
  19.1 0.7 compare_select_fusion
  20.2 3.7 %collective-permute-done.2 = bf16[32,16,128]{2,0,1:T(8,128)(2,1)S(1)} collective-permute-done((bf16[32,16,128]{2,0,1:T(8,128)(2,1)S(1)}, bf16[32,16,128]{2,0,1:T(8,128)(2,1)S(1)}, u32[]{:S(2)}, u32[]{:S(2)}) %collective-permute-start.2) | collective-permute-done | bytes 131104 | tf_op jit(solution)/shard_map/ppermute | solution.py:11
  23.9 3.5 %gather_fusion.4 = bf16[512,32,128]{2,1,0:T(8,128)(2,1)} fusion(bf16[32,128,128]{2,0,1:T(8,128)(2,1)S(1)} %constant_dynamic-update-slice_fusion, s32[1024]{0:T(1024)S(1)} %pad_clamp_fusion), kind=kCustom, calls=%fused_computation.4 | custom fusion | bytes 8390656 | tf_op jit(solution)/shard_map/gather | solution.py:24
  27.4 10.1 %constant_dynamic-update-slice_fusion.9 = (bf16[32,128,128]{2,0,1:T(8,128)(2,1)S(1)}, bf16[32,64,128]{2,0,1:T(8,128)(2,1)S(1)}) fusion(bf16[64,8,128,128]{3,2,1,0:T(8,128)(2,1)} %param.6, bf16[64,8,32,128]{3,2,1,0:T(8,128)(2,1)} %bitcast.67, bf16[64,8]{1,0:T(8,128)(2,1)S(1)} %get-tuple-element.9), kind=kOutput, calls=%fused_computation.34 | convolution fusion | flops 539230208 | bytes 22021120 | tf_op jit(solution)/shard_map/sikc,ikrc->sir/dot_general | solution.py:25
  37.4 0.6 gather_fusion.5
  38.1 0.6 gather_fusion.6
  38.7 0.6 gather_fusion.8
  39.3 0.6 gather_fusion.7
  40.4 2.0 collective-permute-start.7
  42.4 0.7 collective-permute-done.4
  43.1 2.7 collective-permute-done.6
  45.8 2.1 collective-permute-done.7
  48.0 3.6 %gather_fusion.9 = bf16[512,32,128]{2,1,0:T(8,128)(2,1)} fusion(bf16[32,128,128]{2,0,1:T(8,128)(2,1)S(1)} %constant_dynamic-update-slice_fusion.5, s32[1024]{0:T(1024)S(1)} %pad_clamp_fusion), kind=kCustom, calls=%fused_computation.9 | custom fusion | bytes 8390656 | tf_op jit(solution)/shard_map/gather | solution.py:35
  51.5 15.8 %multiply_bitcast_fusion = f32[64,8,128,128]{2,3,1,0:T(8,128)} fusion(f32[64,8]{1,0:T(8,128)S(1)} %get-tuple-element.10, bf16[32,64,8,128]{3,0,2,1:T(8,128)(2,1)} %bitcast.66, bf16[32,64,128]{2,0,1:T(8,128)(2,1)S(1)} %get-tuple-element.12, f32[32]{0:T(128)S(1)} %copy-done.2), kind=kOutput, calls=%fused_computation.10 | convolution fusion | flops 546045952 | bytes 38275200 | tf_op jit(solution)/shard_map/sir,sikc->ikrc/dot_general | solution.py:37
  67.3 33.5 %copy.24 = f32[64,8,128,128]{3,1,0,2:T(8,128)} copy(f32[64,8,128,128]{2,3,1,0:T(8,128)} %multiply_bitcast_fusion) | data formatting | bytes 67108864 | tf_op jit(solution)/shard_map/mul | solution.py:37
  100.8 196.9 %reduce-scatter.2.cloned.1.call-done = f32[64,8,8,128]{3,1,0,2:T(8,128)} async-done(((f32[64,8,128,128]{3,1,0,2:T(8,128)}), f32[64,8,8,128]{3,1,0,2:T(8,128)}) %reduce-scatter.2.cloned.1.call-update) | async-done | bytes 2097168 | tf_op jit(solution)/shard_map/reduce_scatter | solution.py:39
  297.8 4.1 %copy.25 = f32[64,8,8,128]{3,2,1,0:T(8,128)} copy(f32[64,8,8,128]{3,1,0,2:T(8,128)} %reduce-scatter.2.cloned.1.call-done) | data formatting | bytes 4194304 | tf_op jit(solution)/shard_map/reduce_scatter | solution.py:39
  (33 shorter events, 2.3 us)
Async XLA Ops:
  6.5 1.1 copy-start
  6.5 291.2 %reduce-scatter.2.cloned.1.call-start = ((), (), s32[]{:S(2)}) async-start(), calls=%async_computation.1 | async-start | bytes 35651584 | tf_op jit(solution)/shard_map/reduce_scatter | solution.py:39
  8.3 11.6 %collective-permute-start = (bf16[32,16,128]{2,0,1:T(8,128)(2,1)S(1)}, bf16[32,16,128]{2,0,1:T(8,128)(2,1)S(1)}, u32[]{:S(2)}, u32[]{:S(2)}) collective-permute-start(bf16[32,16,128]{2,0,1:T(8,128)(2,1)S(1)} %bitcast.69), channel_id=1, source_target_pairs={{0,224},{16,240},{32,0},{48,16},{64,32},{80,48},{96,64},{112,80},{... | collective-permute-start | bytes 393224 | tf_op jit(solution)/shard_map/ppermute | solution.py:11
  14.8 9.0 %collective-permute-start.3 = (bf16[32,16,128]{2,0,1:T(8,128)(2,1)S(1)}, bf16[32,16,128]{2,0,1:T(8,128)(2,1)S(1)}, u32[]{:S(2)}, u32[]{:S(2)}) collective-permute-start(bf16[32,16,128]{2,0,1:T(8,128)(2,1)S(1)} %bitcast.68), channel_id=1, source_target_pairs={{0,32},{16,48},{32,64},{48,80},{64,96},{80,112},{96,128},{112,144}... | collective-permute-start | bytes 393224 | tf_op jit(solution)/shard_map/ppermute | solution.py:11
  15.5 4.6 %collective-permute-start.1 = (bf16[32,16,128]{2,0,1:T(8,128)(2,1)S(1)}, bf16[32,16,128]{2,0,1:T(8,128)(2,1)S(1)}, u32[]{:S(2)}, u32[]{:S(2)}) collective-permute-start(bf16[32,16,128]{2,0,1:T(8,128)(2,1)S(1)} %bitcast.72), channel_id=1, source_target_pairs={{0,240},{16,0},{32,16},{48,32},{64,48},{80,64},{96,80},{112,96},{1... | collective-permute-start | bytes 393224 | tf_op jit(solution)/shard_map/ppermute | solution.py:11
  18.2 5.6 %collective-permute-start.2 = (bf16[32,16,128]{2,0,1:T(8,128)(2,1)S(1)}, bf16[32,16,128]{2,0,1:T(8,128)(2,1)S(1)}, u32[]{:S(2)}, u32[]{:S(2)}) collective-permute-start(bf16[32,16,128]{2,0,1:T(8,128)(2,1)S(1)} %bitcast.71), channel_id=1, source_target_pairs={{0,16},{16,32},{32,48},{48,64},{64,80},{80,96},{96,112},{112,128},... | collective-permute-start | bytes 393224 | tf_op jit(solution)/shard_map/ppermute | solution.py:11
  38.0 5.0 %collective-permute-start.4 = (bf16[32,16,128]{2,0,1:T(8,128)(2,1)S(1)}, bf16[32,16,128]{2,0,1:T(8,128)(2,1)S(1)}, u32[]{:S(2)}, u32[]{:S(2)}) collective-permute-start(bf16[32,16,128]{2,0,1:T(8,128)(2,1)S(1)} %bitcast.75), channel_id=1, source_target_pairs={{0,224},{16,240},{32,0},{48,16},{64,32},{80,48},{96,64},{112,80},{... | collective-permute-start | bytes 393224 | tf_op jit(solution)/shard_map/ppermute | solution.py:11
  38.7 4.4 %collective-permute-start.5 = (bf16[32,16,128]{2,0,1:T(8,128)(2,1)S(1)}, bf16[32,16,128]{2,0,1:T(8,128)(2,1)S(1)}, u32[]{:S(2)}, u32[]{:S(2)}) collective-permute-start(bf16[32,16,128]{2,0,1:T(8,128)(2,1)S(1)} %bitcast.73), channel_id=1, source_target_pairs={{0,240},{16,0},{32,16},{48,32},{64,48},{80,64},{96,80},{112,96},{1... | collective-permute-start | bytes 393224 | tf_op jit(solution)/shard_map/ppermute | solution.py:11
  39.9 5.9 %collective-permute-start.6 = (bf16[32,16,128]{2,0,1:T(8,128)(2,1)S(1)}, bf16[32,16,128]{2,0,1:T(8,128)(2,1)S(1)}, u32[]{:S(2)}, u32[]{:S(2)}) collective-permute-start(bf16[32,16,128]{2,0,1:T(8,128)(2,1)S(1)} %bitcast.74), channel_id=1, source_target_pairs={{0,16},{16,32},{32,48},{48,64},{64,80},{80,96},{96,112},{112,128},... | collective-permute-start | bytes 393224 | tf_op jit(solution)/shard_map/ppermute | solution.py:11
  40.4 7.6 %collective-permute-start.7 = (bf16[32,16,128]{2,0,1:T(8,128)(2,1)S(1)}, bf16[32,16,128]{2,0,1:T(8,128)(2,1)S(1)}, u32[]{:S(2)}, u32[]{:S(2)}) collective-permute-start(bf16[32,16,128]{2,0,1:T(8,128)(2,1)S(1)} %bitcast.70), channel_id=1, source_target_pairs={{0,32},{16,48},{32,64},{48,80},{64,96},{80,112},{96,128},{112,144}... | collective-permute-start | bytes 393224 | tf_op jit(solution)/shard_map/ppermute | solution.py:11
  48.0 3.6 %copy-start.2 = (f32[32]{0:T(128)S(1)}, f32[32]{0:T(128)}, u32[]{:S(2)}) copy-start(f32[32]{0:T(128)} %param.8) | copy-start | bytes 388
  100.8 201.1 %copy-start.1 = (bf16[32,8192]{1,0:T(8,128)(2,1)S(1)}, bf16[32,8192]{1,0:T(8,128)(2,1)}, u32[]{:S(2)}) copy-start(bf16[32,8192]{1,0:T(8,128)(2,1)} %param.7) | copy-start | bytes 1572868
Sparse Core Ops, SparseCore 0:
  100.9 196.7 reduce-scatter.1
where the time goes:
time: 311 us; the launch traced here: 309 us
  waiting for transfers between devices  206 us (66%)
  local copies, waits for them, and re-layouts  50 us (16%)
  matrix products  25.8 us (8%)
  between operations  13.6 us (4%)
  starting transfers between devices  10.8 us (3%)
    reduce_scatter x1, waiting for transfers between devices, body(): lax.psum_scatter(partial_terms, 'st', scatter_dimension=2, tiled=True)  197 us
    mul x1, local copies, waits for them, and re-layouts, body(): jnp.einsum('sir,sikc->ikrc', weighted, partner, preferred_element_type=jn...  33.5 us
    dot_general x1, matrix products, body(): jnp.einsum('sir,sikc->ikrc', weighted, partner, preferred_element_type=jn...  15.8 us
    ppermute x8, starting transfers between devices, passed_along(): lax.ppermute(value, axis, [(i, (i + by) % count) for i in range(count)])  10.8 us
    dot_general x1, matrix products, body(): jnp.einsum('sikc,ikrc->sir', operand, inv_sqrt_blocks, preferred_element_...  10.1 us
    ppermute x8, waiting for transfers between devices, passed_along(): lax.ppermute(value, axis, [(i, (i + by) % count) for i in range(count)])  9.32 us
  transfers between devices with their start and end apart: 9, of which 6 were waited for; matrix products, arithmetic and copies ran while one was open for 2% of the time, Pallas kernels for 0%

commit v1 on v0

v1 whole, which is shorter than its diff:
```python
import jax
import jax.numpy as jnp
from jax import lax
from jax.experimental import pallas as pl
from jax.experimental.pallas import tpu as pltpu
from jax.sharding import PartitionSpec as P

OFFSETS = (-2, -1, 1, 2)
SIDE = 4
BF16, F32 = jnp.bfloat16, jnp.float32
VMEM_LIMIT = 48 * 1024 * 1024


def params(**more):
    return pltpu.CompilerParams(vmem_limit_bytes=VMEM_LIMIT, **more)


def cost(flops, moved):
    return pl.CostEstimate(flops=flops, bytes_accessed=moved, transcendentals=0)


def along_dom(value, by):
    return lax.ppermute(value, "dom", [(i, (i + by) % 16) for i in range(16)])


def along_x(value, by):
    pairs = [(SIDE * x + y, SIDE * ((x + by) % SIDE) + y) for x in range(SIDE) for y in range(SIDE)]
    return lax.ppermute(value, "st", pairs)


def along_y(value, by):
    pairs = [(SIDE * x + y, SIDE * x + (y + by) % SIDE) for x in range(SIDE) for y in range(SIDE)]
    return lax.ppermute(value, "st", pairs)


def pick_waves(waves, send_list):
    def kernel(send_ref, waves_ref, *outs):
        for n in range(4):
            for j in range(16):
                block = send_ref[n, j]
                outs[n][j] = waves_ref[:, pl.ds(pl.multiple_of(block * 128, 128), 128)]

    piece = jax.ShapeDtypeStruct((16, 32, 128), BF16)
    return pl.pallas_call(
        kernel,
        out_shape=[piece] * 4,
        in_specs=[
            pl.BlockSpec(memory_space=pltpu.SMEM),
            pl.BlockSpec(memory_space=pltpu.VMEM),
        ],
        out_specs=[pl.BlockSpec(memory_space=pltpu.VMEM)] * 4,
        compiler_params=params(),
        name="pick_waves",
    )(send_list, waves)


NT = (((1,), (1,)), ((), ()))
ROWS = 16


def coef_own(inv_sqrt_blocks, waves, block_ref):
    def kernel(ref_ref, blocks_ref, waves_ref, out_ref):
        step = pl.program_id(0)
        for b in range(ROWS):
            i = step * ROWS + b
            operand = jnp.concatenate(
                [
                    waves_ref[:, pl.ds(pl.multiple_of(ref_ref[i, k] * 128, 128), 128)]
                    for k in range(2)
                ],
                axis=1,
            )
            factor = jnp.concatenate([blocks_ref[b, 0], blocks_ref[b, 1]], axis=1)
            out_ref[b] = lax.dot_general(operand, factor, NT, preferred_element_type=F32)

    return pl.pallas_call(
        kernel,
        grid=(64 // ROWS,),
        out_shape=jax.ShapeDtypeStruct((64, 32, 128), F32),
        in_specs=[
            pl.BlockSpec(memory_space=pltpu.SMEM),
            pl.BlockSpec((ROWS, 2, 128, 128), lambda i: (i, 0, 0, 0)),
            pl.BlockSpec((32, 8192), lambda i: (0, 0)),
        ],
        out_specs=pl.BlockSpec((ROWS, 32, 128), lambda i: (i, 0, 0)),
        compiler_params=params(),
        cost_estimate=cost(2 * 64 * 2 * 32 * 128 * 128, 6 * 1024 * 1024),
        name="coef_own",
    )(block_ref, inv_sqrt_blocks, waves)


def coef_all(inv_sqrt_blocks, first, pieces, block_ref, row_count, send_list, occupation):
    def kernel(
        ref_ref, count_ref, send_ref, blocks_ref, first_ref, occ_ref,
        p0, p1, p2, p3, coef_ref, o0, o1, o2, o3, table, total,
    ):
        step, pair = pl.program_id(0), pl.program_id(1)

        @pl.when((step == 0) & (pair == 0))
        def _():
            for n, piece in enumerate((p0, p1, p2, p3)):
                table[16 * n : 16 * n + 16] = piece[...]
            lane = lax.broadcasted_iota(jnp.int32, (32, 128), 1)
            occ = jnp.broadcast_to(occ_ref[...], (32, 128))
            high = occ.astype(BF16).astype(F32)
            middle = (occ - high).astype(BF16).astype(F32)
            low = occ - high - middle
            parts = jnp.where(lane == 0, high, jnp.where(lane == 1, middle, low))
            coef_ref[64] = jnp.where(lane < 3, parts, 0.0).astype(BF16)

        for b in range(ROWS):
            i = step * ROWS + b
            operands = []
            for k in range(2):
                slot = 2 + 2 * pair + k
                code = jnp.clip(ref_ref[i, slot] - 64, 0, 63)
                block = table[code]
                operands.append(jnp.where(slot < count_ref[0, i], block, jnp.zeros_like(block)))
            operand = jnp.concatenate(operands, axis=1)
            factor = jnp.concatenate([blocks_ref[b, 0], blocks_ref[b, 1]], axis=1)
            term = lax.dot_general(operand, factor, NT, preferred_element_type=F32)

            @pl.when(pair == 0)
            def _():
                total[b] = first_ref[b] + term

            @pl.when(pair == 1)
            def _():
                total[b] = total[b] + term

            @pl.when(pair == 2)
            def _():
                coef_ref[i] = (total[b] + term).astype(BF16)

        @pl.when((step == 64 // ROWS - 1) & (pair == 2))
        def _():
            for n, out in enumerate((o0, o1, o2, o3)):
                for j in range(16):
                    out[j] = coef_ref[send_ref[n, j]]

    piece = jax.ShapeDtypeStruct((16, 32, 128), BF16)
    whole = pl.BlockSpec((16, 32, 128), lambda i, k: (0, 0, 0))
    smem = pl.BlockSpec(memory_space=pltpu.SMEM)
    return pl.pallas_call(
        kernel,
        grid=(64 // ROWS, 3),
        out_shape=[jax.ShapeDtypeStruct((65, 32, 128), BF16)] + [piece] * 4,
        in_specs=[
            smem,
            smem,
            smem,
            pl.BlockSpec((ROWS, 2, 128, 128), lambda i, k: (i, k + 1, 0, 0)),
            pl.BlockSpec((ROWS, 32, 128), lambda i, k: (i, 0, 0)),
            pl.BlockSpec((32, 1), lambda i, k: (0, 0)),
        ]
        + [whole] * 4,
        out_specs=[pl.BlockSpec((65, 32, 128), lambda i, k: (0, 0, 0))] + [whole] * 4,
        scratch_shapes=[pltpu.VMEM((64, 32, 128), BF16), pltpu.VMEM((ROWS, 32, 128), F32)],
        compiler_params=params(),
        cost_estimate=cost(2 * 64 * 6 * 32 * 128 * 128, 14 * 1024 * 1024),
        name="coef_all",
    )(block_ref, row_count, send_list, inv_sqrt_blocks, first, occupation, *pieces)


def gathered(value):
    lower_y, lower_x = along_y(value, 1), along_x(value, 1)
    higher_y, higher_x = along_y(value, -1), along_x(value, -1)
    far_y = along_y(lower_y[:32], 1), along_y(higher_y[32:], -1)
    far_x = along_x(lower_x[:32], 1), along_x(higher_x[32:], -1)
    return (lower_y, higher_y, *far_y), (lower_x, higher_x, *far_x)


HALF = jax.ShapeDtypeStruct((4, 32, 16, 128), BF16)
KEPT = jax.ShapeDtypeStruct((4, 32, 16, 128), F32)
PARTS = [KEPT, HALF, HALF, HALF]


def product(weighted, low, high):
    both = jnp.dot(weighted, jnp.concatenate([low, high], axis=1), preferred_element_type=F32)
    for t in range(4):
        rows = both[8 * t : 8 * t + 8]
        yield jnp.concatenate([rows[:, :128], rows[:, 128:]], axis=0)


def density_own(here, coef, gathered_y, gathered_x, block_ref):
    def kernel(here_ref, ref_ref, own, ly, hy, fy0, fy1, lx, hx, fx0, fx1, w_ref, *rest):
        outs, (oy, ox, turned) = rest[:8], rest[8:]
        x, y = here_ref[0], here_ref[1]
        oy[0:32], oy[32:65] = fy0[...], fy1[...]
        ox[0:32], ox[32:65] = fx0[...], fx1[...]
        for v, sources in enumerate(((own, ly, hy, oy), (own, lx, hx, ox))):

            def block_of(c, sources=sources):
                return jnp.concatenate([s[c] for s in sources], axis=0)

            split = block_of(64).astype(F32)
            occ = split[:, 0:1] + split[:, 1:2] + split[:, 2:3]

            def row(i, carry, v=v, occ=occ, block_of=block_of):
                mine = block_of(32 * v + i)
                weighted = (occ * mine.astype(F32)).astype(BF16).astype(F32)
                turned[i % 2] = weighted.T
                groups = []
                for t in range(4):
                    group = SIDE * lax.rem(x + t, SIDE) + y if v == 0 else SIDE * x + lax.rem(y + t, SIDE)
                    groups.append(turned[i % 2, pl.ds(pl.multiple_of(group * 8, 8), 8)])
                lhs = jnp.concatenate(groups, axis=0).astype(BF16)
                w_ref[32 * v + i] = lhs
                other = block_of(jnp.clip(ref_ref[32 * v + i, 1], 0, 63))
                own_block = block_of(jnp.clip(ref_ref[32 * v + i, 0], 0, 63))
                for t, part in enumerate(product(lhs, own_block, other)):
                    outs[4 * v + t][0, i] = part.astype(outs[4 * v + t].dtype)
                return carry

            lax.fori_loop(0, 32, row, 0, unroll=4)

    smem, vmem = pl.BlockSpec(memory_space=pltpu.SMEM), pl.BlockSpec(memory_space=pltpu.VMEM)
    full = pl.BlockSpec((65, 32, 128), lambda i: (0, 0, 0))
    lower = pl.BlockSpec((32, 32, 128), lambda i: (0, 0, 0))
    upper = pl.BlockSpec((33, 32, 128), lambda i: (0, 0, 0))
    return pl.pallas_call(
        kernel,
        grid=(1,),
        out_shape=[jax.ShapeDtypeStruct((64, 32, 128), BF16)] + PARTS * 2,
        in_specs=[smem, smem, full] + [full, full, lower, upper] * 2,
        out_specs=[pl.BlockSpec((64, 32, 128), lambda i: (0, 0, 0))]
        + [pl.BlockSpec((1, 32, 16, 128), lambda i: (0, 0, 0, 0))] * 8,
        scratch_shapes=[
            pltpu.VMEM((65, 32, 128), BF16),
            pltpu.VMEM((65, 32, 128), BF16),
            pltpu.VMEM((2, 128, 128), F32),
        ],
        compiler_params=params(),
        cost_estimate=cost(2 * 64 * 2 * 128 * 32 * 128, 7 * 1024 * 1024),
        name="density_own",
    )(here, block_ref, coef, *gathered_y, *gathered_x)


def density_rest(weighted, halo, halo_y, halo_x, block_ref, begun):
    def kernel(ref_ref, w_ref, own, ly, hy, fy0, fy1, lx, hx, fx0, fx1, *rest):
        outs, (oy, ox) = rest[8:16], rest[16:]
        pair = pl.program_id(0)

        @pl.when(pair == 0)
        def _():
            oy[0:32], oy[32:64] = fy0[...], fy1[...]
            ox[0:32], ox[32:64] = fx0[...], fx1[...]

        for v, sources in enumerate(((own, ly, hy, oy), (own, lx, hx, ox))):

            def block_of(i, slot, sources=sources):
                c = jnp.clip(ref_ref[i, slot] - 64, 0, 63)
                return jnp.concatenate([s[c] for s in sources], axis=0)

            def row(i, carry, v=v, block_of=block_of):
                first = block_of(32 * v + i, 2 + 2 * pair)
                second = block_of(32 * v + i, 3 + 2 * pair)
                for t, part in enumerate(product(w_ref[32 * v + i], first, second)):
                    outs[4 * v + t][0, i] = part.astype(outs[4 * v + t].dtype)
                return carry

            lax.fori_loop(0, 32, row, 0, unroll=8)

    smem = pl.BlockSpec(memory_space=pltpu.SMEM)
    full = pl.BlockSpec((64, 32, 128), lambda i: (0, 0, 0))
    lower = pl.BlockSpec((32, 32, 128), lambda i: (0, 0, 0))
    return pl.pallas_call(
        kernel,
        grid=(3,),
        out_shape=PARTS * 2,
        in_specs=[smem, full, full] + [full, full, lower, lower] * 2 + [pl.BlockSpec(memory_space=pl.ANY)] * 8,
        out_specs=[pl.BlockSpec((1, 32, 16, 128), lambda i: (i + 1, 0, 0, 0))] * 8,
        scratch_shapes=[pltpu.VMEM((64, 32, 128), BF16), pltpu.VMEM((64, 32, 128), BF16)],
        input_output_aliases={11 + n: n for n in range(8)},
        compiler_params=params(),
        cost_estimate=cost(2 * 64 * 6 * 128 * 32 * 128, 10 * 1024 * 1024),
        name="density_rest",
    )(block_ref, weighted, halo, *halo_y, *halo_x, *begun)


def finish(parts, row_count):
    rows = 8

    def kernel(count_ref, *refs):
        ins, out_ref = refs[:8], refs[8]
        step = pl.program_id(0)
        for v in range(2):

            @pl.when(step // (32 // rows) == v)
            def _():
                for pair in range(4):
                    value = ins[4 * v][pair]
                    for t in range(1, 4):
                        value = value + ins[4 * v + t][pair].astype(F32)
                    for b in range(rows):
                        count = count_ref[0, step * rows + b]
                        for k in range(2):
                            part = value[b, 8 * k : 8 * k + 8]
                            out_ref[b, 2 * pair + k] = jnp.where(2 * pair + k < count, part, jnp.zeros_like(part))

    per = 32 // rows
    low = pl.BlockSpec((4, rows, 16, 128), lambda i: (0, jnp.minimum(i, per - 1), 0, 0))
    high = pl.BlockSpec((4, rows, 16, 128), lambda i: (0, jnp.maximum(i - per, 0), 0, 0))
    return pl.pallas_call(
        kernel,
        grid=(64 // rows,),
        out_shape=jax.ShapeDtypeStruct((64, 8, 8, 128), F32),
        in_specs=[pl.BlockSpec(memory_space=pltpu.SMEM)] + [low] * 4 + [high] * 4,
        out_specs=pl.BlockSpec((rows, 8, 8, 128), lambda i: (i, 0, 0, 0)),
        compiler_params=params(),
        cost_estimate=cost(0, 7 * 1024 * 1024),
        name="finish",
    )(row_count, *parts)


def body(inv_sqrt_blocks, waves, occupation, block_ref, row_count, send_list):
    send = send_list[0]
    count = row_count.reshape(1, 64)
    st = lax.axis_index("st")
    here = jnp.stack([st // SIDE, st % SIDE]).astype(jnp.int32)

    picked = pick_waves(waves, send)
    pieces = [along_dom(p, offset) for p, offset in zip(picked, OFFSETS)]
    first = coef_own(inv_sqrt_blocks, waves, block_ref)
    coef, *outgoing = coef_all(
        inv_sqrt_blocks, first, pieces, block_ref, count, send, occupation.reshape(32, 1)
    )
    own_y, own_x = gathered(coef)
    halo = jnp.concatenate([along_dom(p, offset) for p, offset in zip(outgoing, OFFSETS)], axis=0)
    halo_y, halo_x = gathered(halo)
    weighted, *begun = density_own(here, coef, own_y, own_x, block_ref)
    parts = density_rest(weighted, halo, halo_y, halo_x, block_ref, begun)
    arrived = []
    for v, along in enumerate((along_x, along_y)):
        arrived.append(parts[4 * v])
        arrived += [along(parts[4 * v + t], t) for t in range(1, 4)]
    return finish(arrived, count)


def solution(mesh):
    in_specs = (
        P("dom", None, None, None),
        P("st", "dom"),
        P("st"),
        P("dom", None),
        P("dom"),
        P("dom", None, None),
    )
    out_specs = P("dom", None, "st", None)
    return jax.shard_map(body, mesh=mesh, in_specs=in_specs, out_specs=out_specs, check_vma=False)
```

time: 311 us -> 151 us (0.49)
  the two profiles are of different devices: /device:TPU:24 before, /device:TPU:4 now
where the time goes in v1:
time: 151 us
  Pallas kernels  56 us (37%)
  starting transfers between devices  43.7 us (29%)
  waiting for transfers between devices  38.8 us (26%)
  local copies, waits for them, and re-layouts  12.2 us (8%)
    pallas_call x1, Pallas kernels, coef_all(): pl.pallas_call(kernel, grid=(64 // ROWS, 3), out_shape=[jax.ShapeDtypeStr...  31.6 us
    ppermute x11, waiting for transfers between devices, along_x(): return lax.ppermute(value, 'st', pairs)  17.4 us
    ppermute x11, starting transfers between devices, along_x(): return lax.ppermute(value, 'st', pairs)  16.9 us
    ppermute x11, starting transfers between devices, along_y(): return lax.ppermute(value, 'st', pairs)  15.7 us
    ppermute x11, waiting for transfers between devices, along_y(): return lax.ppermute(value, 'st', pairs)  14.6 us
    ppermute x8, starting transfers between devices, along_dom(): return lax.ppermute(value, 'dom', [(i, (i + by) % 16) for i in range(16)])  11.1 us
    pallas_call x1, Pallas kernels, density_own(): pl.pallas_call(kernel, grid=(1,), out_shape=[jax.ShapeDtypeStruct((64, 32...  7.82 us
    unnamed x34, local copies, waits for them, and re-layouts  7.73 us
  transfers between devices with their start and end apart: 30, of which 10 were waited for; matrix products, arithmetic and copies ran while one was open for 4% of the time, Pallas kernels for 8%

profile of v1, /device:TPU:4, one launch (start us, length us, event | category | flops | bytes accessed | tf_op | source)
XLA Modules:
  0.0 151.0 jit_solution(2226987748730916608)
XLA Ops:
  2.5 5.9 %collective-permute-start = (bf16[16,32,128]{2,1,0:T(8,128)(2,1)S(1)}, bf16[16,32,128]{2,1,0:T(8,128)(2,1)S(1)}, u32[]{:S(2)}, u32[]{:S(2)}) collective-permute-start(bf16[16,32,128]{2,1,0:T(8,128)(2,1)S(1)} %get-tuple-element.31), channel_id=1, source_target_pairs={{0,224},{16,240},{32,0},{48,16},{64,32},{80,48},{96,64},{112,80},{... | collective-permute-start | bytes 393224 | tf_op jit(solution)/shard_map/ppermute | solution.py:23
  12.2 3.9 %coef_own.1.first_ref = f32[64,32,128]{2,1,0:T(8,128)S(1)} custom-call(s32[64,8]{1,0:T(8,128)S(1)} %copy.19.ref_ref, bf16[64,8,128,128]{3,2,1,0:T(8,128)(2,1)} %blocks_ref.3, bf16[32,8192]{1,0:T(8,128)(2,1)S(1)} %copy-done.3), custom_call_target="tpu_custom_call" | custom-call | flops 134217728 | bytes 6291456 | tf_op jit(solution)/shard_map/coef_own/pallas_call | solution.py:76
  16.5 31.6 %coef_all.1 = (bf16[65,32,128]{2,1,0:T(8,128)(2,1)S(1)}, bf16[16,32,128]{2,1,0:T(8,128)(2,1)S(1)}, bf16[16,32,128]{2,1,0:T(8,128)(2,1)S(1)}, bf16[16,32,128]{2,1,0:T(8,128)(2,1)S(1)}, bf16[16,32,128]{2,1,0:T(8,128)(2,1)S(1)}) custom-call(s32[64,8]{1,0:T(8,128)S(1)} %copy.19.ref_ref, s32[1,64]{1,0:T(1,128)S(1)} %bitcast.7, s32[4,16]{1,0:T(4,128)S(1)} %bitcast.6, ...), custom_call_target="tpu_custom_call" | custom-call | flops 402653184 | bytes 14680064 | tf_op jit(solution)/shard_map/coef_all/pallas_call | solution.py:144
  48.1 2.3 %collective-permute-start.12 = (bf16[16,32,128]{2,1,0:T(8,128)(2,1)S(1)}, bf16[16,32,128]{2,1,0:T(8,128)(2,1)S(1)}, u32[]{:S(2)}, u32[]{:S(2)}) collective-permute-start(bf16[16,32,128]{2,1,0:T(8,128)(2,1)S(1)} %get-tuple-element.37), channel_id=1, source_target_pairs={{0,224},{16,240},{32,0},{48,16},{64,32},{80,48},{96,64},{112,80},{... | collective-permute-start | bytes 393224 | tf_op jit(solution)/shard_map/ppermute | solution.py:23
  51.5 1.5 collective-permute-start.8
  53.0 3.0 %collective-permute-start.5 = (bf16[65,32,128]{2,1,0:T(8,128)(2,1)S(1)}, bf16[65,32,128]{2,1,0:T(8,128)(2,1)S(1)}, u32[]{:S(2)}, u32[]{:S(2)}) collective-permute-start(bf16[65,32,128]{2,1,0:T(8,128)(2,1)S(1)} %get-tuple-element.35.own), channel_id=1, source_target_pairs={{0,3},{1,0},{2,1},{3,2},{4,7},{5,4},{6,5},{7,6},{8,11},{9,8},{10,9... | collective-permute-start | bytes 1597448 | tf_op jit(solution)/shard_map/ppermute | solution.py:33
  57.2 5.2 %collective-permute-done.14 = bf16[16,32,128]{2,1,0:T(8,128)(2,1)S(1)} collective-permute-done((bf16[16,32,128]{2,1,0:T(8,128)(2,1)S(1)}, bf16[16,32,128]{2,1,0:T(8,128)(2,1)S(1)}, u32[]{:S(2)}, u32[]{:S(2)}) %collective-permute-start.14) | collective-permute-done | bytes 131104 | tf_op jit(solution)/shard_map/ppermute | solution.py:23
  64.7 2.4 %collective-permute-start.20 = (bf16[64,32,128]{2,1,0:T(8,128)(2,1)S(1)}, bf16[64,32,128]{2,1,0:T(8,128)(2,1)S(1)}, u32[]{:S(2)}, u32[]{:S(2)}) collective-permute-start(bf16[64,32,128]{2,1,0:T(8,128)(2,1)S(1)} %constant_dynamic-update-slice_fusion.own), channel_id=1, source_target_pairs={{0,4},{1,5},{2,6},{3,7},{4,8},{5,9},{6,10},{7,11},{8,12},{9,13},{1... | collective-permute-start | bytes 1572872 | tf_op jit(solution)/shard_map/ppermute | solution.py:28
  67.1 3.0 %collective-permute-start.17 = (bf16[64,32,128]{2,1,0:T(8,128)(2,1)S(1)}, bf16[64,32,128]{2,1,0:T(8,128)(2,1)S(1)}, u32[]{:S(2)}, u32[]{:S(2)}) collective-permute-start(bf16[64,32,128]{2,1,0:T(8,128)(2,1)S(1)} %constant_dynamic-update-slice_fusion.own), channel_id=1, source_target_pairs={{0,3},{1,0},{2,1},{3,2},{4,7},{5,4},{6,5},{7,6},{8,11},{9,8},{10,9... | collective-permute-start | bytes 1572872 | tf_op jit(solution)/shard_map/ppermute | solution.py:33
  70.1 7.2 %collective-permute-done.4.ly = bf16[65,32,128]{2,1,0:T(8,128)(2,1)S(1)} collective-permute-done((bf16[65,32,128]{2,1,0:T(8,128)(2,1)S(1)}, bf16[65,32,128]{2,1,0:T(8,128)(2,1)S(1)}, u32[]{:S(2)}, u32[]{:S(2)}) %collective-permute-start.4) | collective-permute-done | bytes 532512 | tf_op jit(solution)/shard_map/ppermute | solution.py:33
  78.8 3.4 %collective-permute-start.10 = (bf16[32,32,128]{2,1,0:T(8,128)(2,1)S(1)}, bf16[32,32,128]{2,1,0:T(8,128)(2,1)S(1)}, u32[]{:S(2)}, u32[]{:S(2)}) collective-permute-start(bf16[32,32,128]{2,1,0:T(8,128)(2,1)S(1)} %slice.34), channel_id=1, source_target_pairs={{0,4},{1,5},{2,6},{3,7},{4,8},{5,9},{6,10},{7,11},{8,12},{9,13},{1... | collective-permute-start | bytes 786440 | tf_op jit(solution)/shard_map/ppermute | solution.py:28
  83.0 3.2 %collective-permute-start.7 = (bf16[33,32,128]{2,1,0:T(8,128)(2,1)}, bf16[33,32,128]{2,1,0:T(8,128)(2,1)S(1)}, u32[]{:S(2)}, u32[]{:S(2)}) collective-permute-start(bf16[33,32,128]{2,1,0:T(8,128)(2,1)} %slice.33), channel_id=1, source_target_pairs={{0,3},{1,0},{2,1},{3,2},{4,7},{5,4},{6,5},{7,6},{8,11},{9,8},{10,9... | collective-permute-start | bytes 811016 | tf_op jit(solution)/shard_map/ppermute | solution.py:33
  89.2 2.9 %collective-permute-start.22 = (bf16[32,32,128]{2,1,0:T(8,128)(2,1)}, bf16[32,32,128]{2,1,0:T(8,128)(2,1)S(1)}, u32[]{:S(2)}, u32[]{:S(2)}) collective-permute-start(bf16[32,32,128]{2,1,0:T(8,128)(2,1)} %slice.38), channel_id=1, source_target_pairs={{0,4},{1,5},{2,6},{3,7},{4,8},{5,9},{6,10},{7,11},{8,12},{9,13},{1... | collective-permute-start | bytes 786440 | tf_op jit(solution)/shard_map/ppermute | solution.py:28
  92.8 2.0 %collective-permute-start.18 = (bf16[32,32,128]{2,1,0:T(8,128)(2,1)}, bf16[32,32,128]{2,1,0:T(8,128)(2,1)}, u32[]{:S(2)}, u32[]{:S(2)}) collective-permute-start(bf16[32,32,128]{2,1,0:T(8,128)(2,1)} %slice.36), channel_id=1, source_target_pairs={{0,1},{1,2},{2,3},{3,0},{4,5},{5,6},{6,7},{7,4},{8,9},{9,10},{10,1... | collective-permute-start | bytes 786440 | tf_op jit(solution)/shard_map/ppermute | solution.py:33
  95.8 7.8 %density_own.1 = (bf16[64,32,128]{2,1,0:T(8,128)(2,1)S(1)}, f32[4,32,16,128]{3,2,1,0:T(8,128)}, bf16[4,32,16,128]{3,2,1,0:T(8,128)(2,1)S(1)}, bf16[4,32,16,128]{...) custom-call(s32[2]{0:T(128)S(1)} %pad_add_fusion.here_ref, ...), custom_call_target="tpu_custom_call" | custom-call | flops 134217728 | bytes 7340032 | tf_op jit(solution)/shard_map/density_own/pallas_call | solution.py:221
  103.7 7.6 %density_rest.1 = (f32[4,32,16,128]{3,2,1,0:T(8,128)}, bf16[4,32,16,128]{3,2,1,0:T(8,128)(2,1)S(1)}, bf16[4,32,16,128]{3,2,1,0:T(8,128)(2,1)S(1)}, bf16[4,32,16,...) custom-call(s32[64,8]{1,0:T(8,128)S(1)} %copy.19.ref_ref, ...), custom_call_target="tpu_custom_call", output_to_operand_aliasing={{0}: (11, {}), {1}: (12, {}), {2}: (13, {}), {3}: (14, {}),... | custom-call | flops 402653184 | bytes 10485760 | tf_op jit(solution)/shard_map/density_rest/pallas_call | solution.py:267
  111.3 3.2 %collective-permute-start.24 = (bf16[4,32,16,128]{3,2,1,0:T(8,128)(2,1)S(1)}, bf16[4,32,16,128]{3,2,1,0:T(8,128)(2,1)S(1)}, u32[]{:S(2)}, u32[]{:S(2)}) collective-permute-start(bf16[4,32,16,128]{3,2,1,0:T(8,128)(2,1)S(1)} %get-tuple-element.50), channel_id=1, source_target_pairs={{0,4},{1,5},{2,6},{3,7},{4,8},{5,9},{6,10},{7,11},{8,12},{9,13},{1... | collective-permute-start | bytes 1572872 | tf_op jit(solution)/shard_map/ppermute | solution.py:28
  114.6 1.5 collective-permute-start.26
  116.1 2.8 %collective-permute-start.28 = (bf16[4,32,16,128]{3,2,1,0:T(8,128)(2,1)S(1)}, bf16[4,32,16,128]{3,2,1,0:T(8,128)(2,1)S(1)}, u32[]{:S(2)}, u32[]{:S(2)}) collective-permute-start(bf16[4,32,16,128]{3,2,1,0:T(8,128)(2,1)S(1)} %get-tuple-element.55), channel_id=1, source_target_pairs={{0,2},{1,3},{2,0},{3,1},{4,6},{5,7},{6,4},{7,5},{8,10},{9,11},{10,... | collective-permute-start | bytes 1572872 | tf_op jit(solution)/shard_map/ppermute | solution.py:33
  118.9 16.2 %collective-permute-done.24.refs_1_ = bf16[4,32,16,128]{3,2,1,0:T(8,128)(2,1)S(1)} collective-permute-done((bf16[4,32,16,128]{3,2,1,0:T(8,128)(2,1)S(1)}, bf16[4,32,16,128]{3,2,1,0:T(8,128)(2,1)S(1)}, u32[]{:S(2)}, u32[]{:S(2)}) %collective-permute-start.24) | collective-permute-done | bytes 524320 | tf_op jit(solution)/shard_map/ppermute | solution.py:28
  135.1 1.6 %collective-permute-start.29 = (bf16[4,32,16,128]{3,2,1,0:T(8,128)(2,1)S(1)}, bf16[4,32,16,128]{3,2,1,0:T(8,128)(2,1)S(1)}, u32[]{:S(2)}, u32[]{:S(2)}) collective-permute-start(bf16[4,32,16,128]{3,2,1,0:T(8,128)(2,1)S(1)} %get-tuple-element.56), channel_id=1, source_target_pairs={{0,3},{1,0},{2,1},{3,2},{4,7},{5,4},{6,5},{7,6},{8,11},{9,8},{10,9... | collective-permute-start | bytes 1572872 | tf_op jit(solution)/shard_map/ppermute | solution.py:33
  136.9 2.0 %collective-permute-done.27.refs_5_ = bf16[4,32,16,128]{3,2,1,0:T(8,128)(2,1)S(1)} collective-permute-done((bf16[4,32,16,128]{3,2,1,0:T(8,128)(2,1)S(1)}, bf16[4,32,16,128]{3,2,1,0:T(8,128)(2,1)S(1)}, u32[]{:S(2)}, u32[]{:S(2)}) %collective-permute-start.27) | collective-permute-done | bytes 524320 | tf_op jit(solution)/shard_map/ppermute | solution.py:33
  138.9 5.4 %collective-permute-done.29.refs_7_ = bf16[4,32,16,128]{3,2,1,0:T(8,128)(2,1)S(1)} collective-permute-done((bf16[4,32,16,128]{3,2,1,0:T(8,128)(2,1)S(1)}, bf16[4,32,16,128]{3,2,1,0:T(8,128)(2,1)S(1)}, u32[]{:S(2)}, u32[]{:S(2)}) %collective-permute-start.29) | collective-permute-done | bytes 524320 | tf_op jit(solution)/shard_map/ppermute | solution.py:33
  146.7 4.3 %finish.1 = f32[64,8,8,128]{3,2,1,0:T(8,128)} custom-call(s32[1,64]{1,0:T(1,128)S(1)} %bitcast.8, f32[4,32,16,128]{3,2,1,0:T(8,128)S(1)} %copy-done, bf16[4,32,16,128]{3,2,1,0:T(8,128)(2,1)S(1)} %collective-permute-done.24.refs_1_, bf16[4,32,16,128]{3,2,1,0:T(8,128)(2,1)S(1)} %collective-permute-done.25.refs_2_, ...), custom_call_target="tpu_custom_call" | custom-call | bytes 7340032 | tf_op jit(solution)/shard_map/finish/pallas_call | solution.py:304
  (87 shorter events, 20.7 us)
Async XLA Ops:
  2.5 13.6 %collective-permute-start = (bf16[16,32,128]{2,1,0:T(8,128)(2,1)S(1)}, bf16[16,32,128]{2,1,0:T(8,128)(2,1)S(1)}, u32[]{:S(2)}, u32[]{:S(2)}) collective-permute-start(bf16[16,32,128]{2,1,0:T(8,128)(2,1)S(1)} %get-tuple-element.31), channel_id=1, source_target_pairs={{0,224},{16,240},{32,0},{48,16},{64,32},{80,48},{96,64},{112,80},{... | collective-permute-start | bytes 393224 | tf_op jit(solution)/shard_map/ppermute | solution.py:23
  48.1 7.9 %collective-permute-start.12 = (bf16[16,32,128]{2,1,0:T(8,128)(2,1)S(1)}, bf16[16,32,128]{2,1,0:T(8,128)(2,1)S(1)}, u32[]{:S(2)}, u32[]{:S(2)}) collective-permute-start(bf16[16,32,128]{2,1,0:T(8,128)(2,1)S(1)} %get-tuple-element.37), channel_id=1, source_target_pairs={{0,224},{16,240},{32,0},{48,16},{64,32},{80,48},{96,64},{112,80},{... | collective-permute-start | bytes 393224 | tf_op jit(solution)/shard_map/ppermute | solution.py:23
  50.4 14.2 %collective-permute-start.9 = (bf16[65,32,128]{2,1,0:T(8,128)(2,1)S(1)}, bf16[65,32,128]{2,1,0:T(8,128)(2,1)S(1)}, u32[]{:S(2)}, u32[]{:S(2)}) collective-permute-start(bf16[65,32,128]{2,1,0:T(8,128)(2,1)S(1)} %get-tuple-element.35.own), channel_id=1, source_target_pairs={{0,12},{1,13},{2,14},{3,15},{4,0},{5,1},{6,2},{7,3},{8,4},{9,5},{1... | collective-permute-start | bytes 1597448 | tf_op jit(solution)/shard_map/ppermute | solution.py:28
  51.5 15.5 %collective-permute-start.8 = (bf16[65,32,128]{2,1,0:T(8,128)(2,1)S(1)}, bf16[65,32,128]{2,1,0:T(8,128)(2,1)S(1)}, u32[]{:S(2)}, u32[]{:S(2)}) collective-permute-start(bf16[65,32,128]{2,1,0:T(8,128)(2,1)S(1)} %get-tuple-element.35.own), channel_id=1, source_target_pairs={{0,4},{1,5},{2,6},{3,7},{4,8},{5,9},{6,10},{7,11},{8,12},{9,13},{1... | collective-permute-start | bytes 1597448 | tf_op jit(solution)/shard_map/ppermute | solution.py:28
  53.0 17.1 %collective-permute-start.5 = (bf16[65,32,128]{2,1,0:T(8,128)(2,1)S(1)}, bf16[65,32,128]{2,1,0:T(8,128)(2,1)S(1)}, u32[]{:S(2)}, u32[]{:S(2)}) collective-permute-start(bf16[65,32,128]{2,1,0:T(8,128)(2,1)S(1)} %get-tuple-element.35.own), channel_id=1, source_target_pairs={{0,3},{1,0},{2,1},{3,2},{4,7},{5,4},{6,5},{7,6},{8,11},{9,8},{10,9... | collective-permute-start | bytes 1597448 | tf_op jit(solution)/shard_map/ppermute | solution.py:33
  62.4 14.9 %collective-permute-start.4 = (bf16[65,32,128]{2,1,0:T(8,128)(2,1)S(1)}, bf16[65,32,128]{2,1,0:T(8,128)(2,1)S(1)}, u32[]{:S(2)}, u32[]{:S(2)}) collective-permute-start(bf16[65,32,128]{2,1,0:T(8,128)(2,1)S(1)} %get-tuple-element.35.own), channel_id=1, source_target_pairs={{0,1},{1,2},{2,3},{3,0},{4,5},{5,6},{6,7},{7,4},{8,9},{9,10},{10,1... | collective-permute-start | bytes 1597448 | tf_op jit(solution)/shard_map/ppermute | solution.py:33
  63.7 15.1 %collective-permute-start.21 = (bf16[64,32,128]{2,1,0:T(8,128)(2,1)S(1)}, bf16[64,32,128]{2,1,0:T(8,128)(2,1)S(1)}, u32[]{:S(2)}, u32[]{:S(2)}) collective-permute-start(bf16[64,32,128]{2,1,0:T(8,128)(2,1)S(1)} %constant_dynamic-update-slice_fusion.own), channel_id=1, source_target_pairs={{0,12},{1,13},{2,14},{3,15},{4,0},{5,1},{6,2},{7,3},{8,4},{9,5},{1... | collective-permute-start | bytes 1572872 | tf_op jit(solution)/shard_map/ppermute | solution.py:28
  64.7 17.5 %collective-permute-start.20 = (bf16[64,32,128]{2,1,0:T(8,128)(2,1)S(1)}, bf16[64,32,128]{2,1,0:T(8,128)(2,1)S(1)}, u32[]{:S(2)}, u32[]{:S(2)}) collective-permute-start(bf16[64,32,128]{2,1,0:T(8,128)(2,1)S(1)} %constant_dynamic-update-slice_fusion.own), channel_id=1, source_target_pairs={{0,4},{1,5},{2,6},{3,7},{4,8},{5,9},{6,10},{7,11},{8,12},{9,13},{1... | collective-permute-start | bytes 1572872 | tf_op jit(solution)/shard_map/ppermute | solution.py:28
  67.1 15.9 %collective-permute-start.17 = (bf16[64,32,128]{2,1,0:T(8,128)(2,1)S(1)}, bf16[64,32,128]{2,1,0:T(8,128)(2,1)S(1)}, u32[]{:S(2)}, u32[]{:S(2)}) collective-permute-start(bf16[64,32,128]{2,1,0:T(8,128)(2,1)S(1)} %constant_dynamic-update-slice_fusion.own), channel_id=1, source_target_pairs={{0,3},{1,0},{2,1},{3,2},{4,7},{5,4},{6,5},{7,6},{8,11},{9,8},{10,9... | collective-permute-start | bytes 1572872 | tf_op jit(solution)/shard_map/ppermute | solution.py:33
  70.1 18.3 %collective-permute-start.16 = (bf16[64,32,128]{2,1,0:T(8,128)(2,1)S(1)}, bf16[64,32,128]{2,1,0:T(8,128)(2,1)S(1)}, u32[]{:S(2)}, u32[]{:S(2)}) collective-permute-start(bf16[64,32,128]{2,1,0:T(8,128)(2,1)S(1)} %constant_dynamic-update-slice_fusion.own), channel_id=1, source_target_pairs={{0,1},{1,2},{2,3},{3,0},{4,5},{5,6},{6,7},{7,4},{8,9},{9,10},{10,1... | collective-permute-start | bytes 1572872 | tf_op jit(solution)/shard_map/ppermute | solution.py:33
  77.3 15.4 %collective-permute-start.11 = (bf16[33,32,128]{2,1,0:T(8,128)(2,1)S(1)}, bf16[33,32,128]{2,1,0:T(8,128)(2,1)S(1)}, u32[]{:S(2)}, u32[]{:S(2)}) collective-permute-start(bf16[33,32,128]{2,1,0:T(8,128)(2,1)S(1)} %slice.35), channel_id=1, source_target_pairs={{0,12},{1,13},{2,14},{3,15},{4,0},{5,1},{6,2},{7,3},{8,4},{9,5},{1... | collective-permute-start | bytes 811016 | tf_op jit(solution)/shard_map/ppermute | solution.py:28
  78.8 10.4 %collective-permute-start.10 = (bf16[32,32,128]{2,1,0:T(8,128)(2,1)S(1)}, bf16[32,32,128]{2,1,0:T(8,128)(2,1)S(1)}, u32[]{:S(2)}, u32[]{:S(2)}) collective-permute-start(bf16[32,32,128]{2,1,0:T(8,128)(2,1)S(1)} %slice.34), channel_id=1, source_target_pairs={{0,4},{1,5},{2,6},{3,7},{4,8},{5,9},{6,10},{7,11},{8,12},{9,13},{1... | collective-permute-start | bytes 786440 | tf_op jit(solution)/shard_map/ppermute | solution.py:28
  82.2 9.9 %collective-permute-start.6 = (bf16[32,32,128]{2,1,0:T(8,128)(2,1)S(1)}, bf16[32,32,128]{2,1,0:T(8,128)(2,1)S(1)}, u32[]{:S(2)}, u32[]{:S(2)}) collective-permute-start(bf16[32,32,128]{2,1,0:T(8,128)(2,1)S(1)} %slice.32), channel_id=1, source_target_pairs={{0,1},{1,2},{2,3},{3,0},{4,5},{5,6},{6,7},{7,4},{8,9},{9,10},{10,1... | collective-permute-start | bytes 786440 | tf_op jit(solution)/shard_map/ppermute | solution.py:33
  83.0 11.9 %collective-permute-start.7 = (bf16[33,32,128]{2,1,0:T(8,128)(2,1)}, bf16[33,32,128]{2,1,0:T(8,128)(2,1)S(1)}, u32[]{:S(2)}, u32[]{:S(2)}) collective-permute-start(bf16[33,32,128]{2,1,0:T(8,128)(2,1)} %slice.33), channel_id=1, source_target_pairs={{0,3},{1,0},{2,1},{3,2},{4,7},{5,4},{6,5},{7,6},{8,11},{9,8},{10,9... | collective-permute-start | bytes 811016 | tf_op jit(solution)/shard_map/ppermute | solution.py:33
  88.4 15.3 %collective-permute-start.23 = (bf16[32,32,128]{2,1,0:T(8,128)(2,1)}, bf16[32,32,128]{2,1,0:T(8,128)(2,1)S(1)}, u32[]{:S(2)}, u32[]{:S(2)}) collective-permute-start(bf16[32,32,128]{2,1,0:T(8,128)(2,1)} %slice.39), channel_id=1, source_target_pairs={{0,12},{1,13},{2,14},{3,15},{4,0},{5,1},{6,2},{7,3},{8,4},{9,5},{1... | collective-permute-start | bytes 786440 | tf_op jit(solution)/shard_map/ppermute | solution.py:28
  89.2 14.5 %collective-permute-start.22 = (bf16[32,32,128]{2,1,0:T(8,128)(2,1)}, bf16[32,32,128]{2,1,0:T(8,128)(2,1)S(1)}, u32[]{:S(2)}, u32[]{:S(2)}) collective-permute-start(bf16[32,32,128]{2,1,0:T(8,128)(2,1)} %slice.38), channel_id=1, source_target_pairs={{0,4},{1,5},{2,6},{3,7},{4,8},{5,9},{6,10},{7,11},{8,12},{9,13},{1... | collective-permute-start | bytes 786440 | tf_op jit(solution)/shard_map/ppermute | solution.py:28
  92.8 10.9 %collective-permute-start.19 = (bf16[32,32,128]{2,1,0:T(8,128)(2,1)}, bf16[32,32,128]{2,1,0:T(8,128)(2,1)}, u32[]{:S(2)}, u32[]{:S(2)}) collective-permute-start(bf16[32,32,128]{2,1,0:T(8,128)(2,1)} %slice.37), channel_id=1, source_target_pairs={{0,3},{1,0},{2,1},{3,2},{4,7},{5,4},{6,5},{7,6},{8,11},{9,8},{10,9... | collective-permute-start | bytes 786440 | tf_op jit(solution)/shard_map/ppermute | solution.py:33
  92.8 10.9 %collective-permute-start.18 = (bf16[32,32,128]{2,1,0:T(8,128)(2,1)}, bf16[32,32,128]{2,1,0:T(8,128)(2,1)}, u32[]{:S(2)}, u32[]{:S(2)}) collective-permute-start(bf16[32,32,128]{2,1,0:T(8,128)(2,1)} %slice.36), channel_id=1, source_target_pairs={{0,1},{1,2},{2,3},{3,0},{4,5},{5,6},{6,7},{7,4},{8,9},{9,10},{10,1... | collective-permute-start | bytes 786440 | tf_op jit(solution)/shard_map/ppermute | solution.py:33
  111.3 23.8 %collective-permute-start.24 = (bf16[4,32,16,128]{3,2,1,0:T(8,128)(2,1)S(1)}, bf16[4,32,16,128]{3,2,1,0:T(8,128)(2,1)S(1)}, u32[]{:S(2)}, u32[]{:S(2)}) collective-permute-start(bf16[4,32,16,128]{3,2,1,0:T(8,128)(2,1)S(1)} %get-tuple-element.50), channel_id=1, source_target_pairs={{0,4},{1,5},{2,6},{3,7},{4,8},{5,9},{6,10},{7,11},{8,12},{9,13},{1... | collective-permute-start | bytes 1572872 | tf_op jit(solution)/shard_map/ppermute | solution.py:28
  114.6 22.1 %collective-permute-start.25 = (bf16[4,32,16,128]{3,2,1,0:T(8,128)(2,1)S(1)}, bf16[4,32,16,128]{3,2,1,0:T(8,128)(2,1)S(1)}, u32[]{:S(2)}, u32[]{:S(2)}) collective-permute-start(bf16[4,32,16,128]{3,2,1,0:T(8,128)(2,1)S(1)} %get-tuple-element.51), channel_id=1, source_target_pairs={{0,8},{1,9},{2,10},{3,11},{4,12},{5,13},{6,14},{7,15},{8,0},{9,1},... | collective-permute-start | bytes 1572872 | tf_op jit(solution)/shard_map/ppermute | solution.py:28
  114.6 22.4 %collective-permute-start.26 = (bf16[4,32,16,128]{3,2,1,0:T(8,128)(2,1)S(1)}, bf16[4,32,16,128]{3,2,1,0:T(8,128)(2,1)S(1)}, u32[]{:S(2)}, u32[]{:S(2)}) collective-permute-start(bf16[4,32,16,128]{3,2,1,0:T(8,128)(2,1)S(1)} %get-tuple-element.52), channel_id=1, source_target_pairs={{0,12},{1,13},{2,14},{3,15},{4,0},{5,1},{6,2},{7,3},{8,4},{9,5},{1... | collective-permute-start | bytes 1572872 | tf_op jit(solution)/shard_map/ppermute | solution.py:28
  116.1 22.8 %collective-permute-start.27 = (bf16[4,32,16,128]{3,2,1,0:T(8,128)(2,1)S(1)}, bf16[4,32,16,128]{3,2,1,0:T(8,128)(2,1)S(1)}, u32[]{:S(2)}, u32[]{:S(2)}) collective-permute-start(bf16[4,32,16,128]{3,2,1,0:T(8,128)(2,1)S(1)} %get-tuple-element.54), channel_id=1, source_target_pairs={{0,1},{1,2},{2,3},{3,0},{4,5},{5,6},{6,7},{7,4},{8,9},{9,10},{10,1... | collective-permute-start | bytes 1572872 | tf_op jit(solution)/shard_map/ppermute | solution.py:33
  116.1 22.8 %collective-permute-start.28 = (bf16[4,32,16,128]{3,2,1,0:T(8,128)(2,1)S(1)}, bf16[4,32,16,128]{3,2,1,0:T(8,128)(2,1)S(1)}, u32[]{:S(2)}, u32[]{:S(2)}) collective-permute-start(bf16[4,32,16,128]{3,2,1,0:T(8,128)(2,1)S(1)} %get-tuple-element.55), channel_id=1, source_target_pairs={{0,2},{1,3},{2,0},{3,1},{4,6},{5,7},{6,4},{7,5},{8,10},{9,11},{10,... | collective-permute-start | bytes 1572872 | tf_op jit(solution)/shard_map/ppermute | solution.py:33
  135.1 9.2 %collective-permute-start.29 = (bf16[4,32,16,128]{3,2,1,0:T(8,128)(2,1)S(1)}, bf16[4,32,16,128]{3,2,1,0:T(8,128)(2,1)S(1)}, u32[]{:S(2)}, u32[]{:S(2)}) collective-permute-start(bf16[4,32,16,128]{3,2,1,0:T(8,128)(2,1)S(1)} %get-tuple-element.56), channel_id=1, source_target_pairs={{0,3},{1,0},{2,1},{3,2},{4,7},{5,4},{6,5},{7,6},{8,11},{9,8},{10,9... | collective-permute-start | bytes 1572872 | tf_op jit(solution)/shard_map/ppermute | solution.py:33
  (21 other events, 164.5 us)

commit v2 on v1

--- a/solution.py
+++ b/solution.py
@@ -8,7 +8,7 @@
 OFFSETS = (-2, -1, 1, 2)
 SIDE = 4
 BF16, F32 = jnp.bfloat16, jnp.float32
-VMEM_LIMIT = 48 * 1024 * 1024
+VMEM_LIMIT = 32 * 1024 * 1024
 
 
 def params(**more):
@@ -56,13 +56,14 @@
 
 NT = (((1,), (1,)), ((), ()))
 ROWS = 16
+OWN_ROWS = 32
 
 
 def coef_own(inv_sqrt_blocks, waves, block_ref):
     def kernel(ref_ref, blocks_ref, waves_ref, out_ref):
         step = pl.program_id(0)
-        for b in range(ROWS):
-            i = step * ROWS + b
+        for b in range(OWN_ROWS):
+            i = step * OWN_ROWS + b
             operand = jnp.concatenate(
                 [
                     waves_ref[:, pl.ds(pl.multiple_of(ref_ref[i, k] * 128, 128), 128)]
@@ -75,14 +76,14 @@
 
     return pl.pallas_call(
         kernel,
-        grid=(64 // ROWS,),
+        grid=(64 // OWN_ROWS,),
         out_shape=jax.ShapeDtypeStruct((64, 32, 128), F32),
         in_specs=[
             pl.BlockSpec(memory_space=pltpu.SMEM),
-            pl.BlockSpec((ROWS, 2, 128, 128), lambda i: (i, 0, 0, 0)),
+            pl.BlockSpec((OWN_ROWS, 2, 128, 128), lambda i: (i, 0, 0, 0)),
             pl.BlockSpec((32, 8192), lambda i: (0, 0)),
         ],
-        out_specs=pl.BlockSpec((ROWS, 32, 128), lambda i: (i, 0, 0)),
+        out_specs=pl.BlockSpec((OWN_ROWS, 32, 128), lambda i: (i, 0, 0)),
         compiler_params=params(),
         cost_estimate=cost(2 * 64 * 2 * 32 * 128 * 128, 6 * 1024 * 1024),
         name="coef_own",
@@ -91,12 +92,12 @@
 
 def coef_all(inv_sqrt_blocks, first, pieces, block_ref, row_count, send_list, occupation):
     def kernel(
-        ref_ref, count_ref, send_ref, blocks_ref, first_ref, occ_ref,
-        p0, p1, p2, p3, coef_ref, o0, o1, o2, o3, table, total,
+        ref_ref, count_ref, send_ref, blocks_1, blocks_2, blocks_3, first_ref, occ_ref,
+        p0, p1, p2, p3, coef_ref, o0, o1, o2, o3, table,
     ):
-        step, pair = pl.program_id(0), pl.program_id(1)
-
-        @pl.when((step == 0) & (pair == 0))
+        step = pl.program_id(0)
+
+        @pl.when(step == 0)
         def _():
             for n, piece in enumerate((p0, p1, p2, p3)):
                 table[16 * n : 16 * n + 16] = piece[...]
@@ -110,64 +111,67 @@
 
         for b in range(ROWS):
             i = step * ROWS + b
-            operands = []
-            for k in range(2):
-                slot = 2 + 2 * pair + k
-                code = jnp.clip(ref_ref[i, slot] - 64, 0, 63)
-                block = table[code]
+            operands, factors = [], []
+            for slot in range(2, 8):
+                block = table[jnp.clip(ref_ref[i, slot] - 64, 0, 63)]
                 operands.append(jnp.where(slot < count_ref[0, i], block, jnp.zeros_like(block)))
-            operand = jnp.concatenate(operands, axis=1)
-            factor = jnp.concatenate([blocks_ref[b, 0], blocks_ref[b, 1]], axis=1)
-            term = lax.dot_general(operand, factor, NT, preferred_element_type=F32)
-
-            @pl.when(pair == 0)
-            def _():
-                total[b] = first_ref[b] + term
-
-            @pl.when(pair == 1)
-            def _():
-                total[b] = total[b] + term
-
-            @pl.when(pair == 2)
-            def _():
-                coef_ref[i] = (total[b] + term).astype(BF16)
-
-        @pl.when((step == 64 // ROWS - 1) & (pair == 2))
+                factors.append((blocks_1, blocks_2, blocks_3)[slot // 2 - 1][b, slot % 2])
+            term = lax.dot_general(
+                jnp.concatenate(factors, axis=1),
+                jnp.concatenate(operands, axis=1),
+                NT,
+                preferred_element_type=F32,
+            )
+            coef_ref[i] = (first_ref[b] + term.T).astype(BF16)
+
+        @pl.when(step == 64 // ROWS - 1)
         def _():
             for n, out in enumerate((o0, o1, o2, o3)):
                 for j in range(16):
                     out[j] = coef_ref[send_ref[n, j]]
 
     piece = jax.ShapeDtypeStruct((16, 32, 128), BF16)
-    whole = pl.BlockSpec((16, 32, 128), lambda i, k: (0, 0, 0))
+    whole = pl.BlockSpec((16, 32, 128), lambda i: (0, 0, 0))
     smem = pl.BlockSpec(memory_space=pltpu.SMEM)
     return pl.pallas_call(
         kernel,
-        grid=(64 // ROWS, 3),
+        grid=(64 // ROWS,),
         out_shape=[jax.ShapeDtypeStruct((65, 32, 128), BF16)] + [piece] * 4,
-        in_specs=[
-            smem,
-            smem,
-            smem,
-            pl.BlockSpec((ROWS, 2, 128, 128), lambda i, k: (i, k + 1, 0, 0)),
-            pl.BlockSpec((ROWS, 32, 128), lambda i, k: (i, 0, 0)),
-            pl.BlockSpec((32, 1), lambda i, k: (0, 0)),
+        in_specs=[smem, smem, smem]
+        + [pl.BlockSpec((ROWS, 2, 128, 128), lambda i, k=k: (i, k, 0, 0)) for k in (1, 2, 3)]
+        + [
+            pl.BlockSpec((ROWS, 32, 128), lambda i: (i, 0, 0)),
+            pl.BlockSpec((32, 1), lambda i: (0, 0)),
         ]
         + [whole] * 4,
-        out_specs=[pl.BlockSpec((65, 32, 128), lambda i, k: (0, 0, 0))] + [whole] * 4,
-        scratch_shapes=[pltpu.VMEM((64, 32, 128), BF16), pltpu.VMEM((ROWS, 32, 128), F32)],
+        out_specs=[pl.BlockSpec((65, 32, 128), lambda i: (0, 0, 0))] + [whole] * 4,
+        scratch_shapes=[pltpu.VMEM((64, 32, 128), BF16)],
         compiler_params=params(),
         cost_estimate=cost(2 * 64 * 6 * 32 * 128 * 128, 14 * 1024 * 1024),
         name="coef_all",
-    )(block_ref, row_count, send_list, inv_sqrt_blocks, first, occupation, *pieces)
-
-
-def gathered(value):
-    lower_y, lower_x = along_y(value, 1), along_x(value, 1)
-    higher_y, higher_x = along_y(value, -1), along_x(value, -1)
+    )(
+        block_ref, row_count, send_list, inv_sqrt_blocks, inv_sqrt_blocks, inv_sqrt_blocks,
+        first, occupation, *pieces,
+    )
+
+
+def from_beside(value):
+    return along_y(value, 1), along_y(value, -1), along_x(value, 1), along_x(value, -1)
+
+
+def from_far(beside):
+    lower_y, higher_y, lower_x, higher_x = beside
     far_y = along_y(lower_y[:32], 1), along_y(higher_y[32:], -1)
     far_x = along_x(lower_x[:32], 1), along_x(higher_x[32:], -1)
     return (lower_y, higher_y, *far_y), (lower_x, higher_x, *far_x)
+
+
+def unite(table, pieces):
+    own, lower, higher, far_0, far_1 = pieces
+    for n, piece in enumerate((own, lower, higher)):
+        table[:, 32 * n : 32 * n + 32] = piece[...]
+    table[0:32, 96:128] = far_0[...]
+    table[32 : table.shape[0], 96:128] = far_1[...]
 
 
 HALF = jax.ShapeDtypeStruct((4, 32, 16, 128), BF16)
@@ -184,35 +188,29 @@
 
 def density_own(here, coef, gathered_y, gathered_x, block_ref):
     def kernel(here_ref, ref_ref, own, ly, hy, fy0, fy1, lx, hx, fx0, fx1, w_ref, *rest):
-        outs, (oy, ox, turned) = rest[:8], rest[8:]
+        outs, tables, turned = rest[:8], rest[8:10], rest[10]
         x, y = here_ref[0], here_ref[1]
-        oy[0:32], oy[32:65] = fy0[...], fy1[...]
-        ox[0:32], ox[32:65] = fx0[...], fx1[...]
-        for v, sources in enumerate(((own, ly, hy, oy), (own, lx, hx, ox))):
-
-            def block_of(c, sources=sources):
-                return jnp.concatenate([s[c] for s in sources], axis=0)
-
-            split = block_of(64).astype(F32)
+        for v, pieces in enumerate(((own, ly, hy, fy0, fy1), (own, lx, hx, fx0, fx1))):
+            table = tables[v]
+            unite(table, pieces)
+            split = table[64].astype(F32)
             occ = split[:, 0:1] + split[:, 1:2] + split[:, 2:3]
 
-            def row(i, carry, v=v, occ=occ, block_of=block_of):
-                mine = block_of(32 * v + i)
+            for i in range(32):
+                mine = table[32 * v + i]
                 weighted = (occ * mine.astype(F32)).astype(BF16).astype(F32)
-                turned[i % 2] = weighted.T
+                turned[32 * v + i] = weighted.T
+
+            for i in range(32):
                 groups = []
                 for t in range(4):
                     group = SIDE * lax.rem(x + t, SIDE) + y if v == 0 else SIDE * x + lax.rem(y + t, SIDE)
-                    groups.append(turned[i % 2, pl.ds(pl.multiple_of(group * 8, 8), 8)])
+                    groups.append(turned[32 * v + i, pl.ds(pl.multiple_of(group * 8, 8), 8)])
                 lhs = jnp.concatenate(groups, axis=0).astype(BF16)
                 w_ref[32 * v + i] = lhs
-                other = block_of(jnp.clip(ref_ref[32 * v + i, 1], 0, 63))
-                own_block = block_of(jnp.clip(ref_ref[32 * v + i, 0], 0, 63))
-                for t, part in enumerate(product(lhs, own_block, other)):
+                both = [table[jnp.clip(ref_ref[32 * v + i, k], 0, 63)] for k in range(2)]
+                for t, part in enumerate(product(lhs, *both)):
                     outs[4 * v + t][0, i] = part.astype(outs[4 * v + t].dtype)
-                return carry
-
-            lax.fori_loop(0, 32, row, 0, unroll=4)
 
     smem, vmem = pl.BlockSpec(memory_space=pltpu.SMEM), pl.BlockSpec(memory_space=pltpu.VMEM)
     full = pl.BlockSpec((65, 32, 128), lambda i: (0, 0, 0))
@@ -226,9 +224,9 @@
         out_specs=[pl.BlockSpec((64, 32, 128), lambda i: (0, 0, 0))]
         + [pl.BlockSpec((1, 32, 16, 128), lambda i: (0, 0, 0, 0))] * 8,
         scratch_shapes=[
-            pltpu.VMEM((65, 32, 128), BF16),
-            pltpu.VMEM((65, 32, 128), BF16),
-            pltpu.VMEM((2, 128, 128), F32),
+            pltpu.VMEM((65, 128, 128), BF16),
+            pltpu.VMEM((65, 128, 128), BF16),
+            pltpu.VMEM((64, 128, 128), F32),
         ],
         compiler_params=params(),
         cost_estimate=cost(2 * 64 * 2 * 128 * 32 * 128, 7 * 1024 * 1024),
@@ -238,28 +236,20 @@
 
 def density_rest(weighted, halo, halo_y, halo_x, block_ref, begun):
     def kernel(ref_ref, w_ref, own, ly, hy, fy0, fy1, lx, hx, fx0, fx1, *rest):
-        outs, (oy, ox) = rest[8:16], rest[16:]
+        outs, tables = rest[8:16], rest[16:]
         pair = pl.program_id(0)
 
         @pl.when(pair == 0)
         def _():
-            oy[0:32], oy[32:64] = fy0[...], fy1[...]
-            ox[0:32], ox[32:64] = fx0[...], fx1[...]
-
-        for v, sources in enumerate(((own, ly, hy, oy), (own, lx, hx, ox))):
-
-            def block_of(i, slot, sources=sources):
-                c = jnp.clip(ref_ref[i, slot] - 64, 0, 63)
-                return jnp.concatenate([s[c] for s in sources], axis=0)
-
-            def row(i, carry, v=v, block_of=block_of):
-                first = block_of(32 * v + i, 2 + 2 * pair)
-                second = block_of(32 * v + i, 3 + 2 * pair)
-                for t, part in enumerate(product(w_ref[32 * v + i], first, second)):
+            unite(tables[0], (own, ly, hy, fy0, fy1))
+            unite(tables[1], (own, lx, hx, fx0, fx1))
+
+        for v, table in enumerate(tables):
+            for i in range(32):
+                codes = [ref_ref[32 * v + i, 2 + 2 * pair + k] - 64 for k in range(2)]
+                both = [table[jnp.clip(code, 0, 63)] for code in codes]
+                for t, part in enumerate(product(w_ref[32 * v + i], *both)):
                     outs[4 * v + t][0, i] = part.astype(outs[4 * v + t].dtype)
-                return carry
-
-            lax.fori_loop(0, 32, row, 0, unroll=8)
 
     smem = pl.BlockSpec(memory_space=pltpu.SMEM)
     full = pl.BlockSpec((64, 32, 128), lambda i: (0, 0, 0))
@@ -270,7 +260,7 @@
         out_shape=PARTS * 2,
         in_specs=[smem, full, full] + [full, full, lower, lower] * 2 + [pl.BlockSpec(memory_space=pl.ANY)] * 8,
         out_specs=[pl.BlockSpec((1, 32, 16, 128), lambda i: (i + 1, 0, 0, 0))] * 8,
-        scratch_shapes=[pltpu.VMEM((64, 32, 128), BF16), pltpu.VMEM((64, 32, 128), BF16)],
+        scratch_shapes=[pltpu.VMEM((64, 128, 128), BF16)] * 2,
         input_output_aliases={11 + n: n for n in range(8)},
         compiler_params=params(),
         cost_estimate=cost(2 * 64 * 6 * 128 * 32 * 128, 10 * 1024 * 1024),
@@ -279,7 +269,7 @@
 
 
 def finish(parts, row_count):
-    rows = 8
+    rows = 16
 
     def kernel(count_ref, *refs):
         ins, out_ref = refs[:8], refs[8]
@@ -325,9 +315,13 @@
     coef, *outgoing = coef_all(
         inv_sqrt_blocks, first, pieces, block_ref, count, send, occupation.reshape(32, 1)
     )
-    own_y, own_x = gathered(coef)
-    halo = jnp.concatenate([along_dom(p, offset) for p, offset in zip(outgoing, OFFSETS)], axis=0)
-    halo_y, halo_x = gathered(halo)
+    beside = from_beside(coef)
+    halos = [along_dom(p, offset) for p, offset in zip(outgoing[:2], OFFSETS)]
+    *beside, third, fourth = lax.optimization_barrier((*beside, *outgoing[2:]))
+    halos += [along_dom(p, offset) for p, offset in zip((third, fourth), OFFSETS[2:])]
+    own_y, own_x = from_far(beside)
+    halo = jnp.concatenate(halos, axis=0)
+    halo_y, halo_x = from_far(from_beside(halo))
     weighted, *begun = density_own(here, coef, own_y, own_x, block_ref)
     parts = density_rest(weighted, halo, halo_y, halo_x, block_ref, begun)
     arrived = []

time: 151 us -> 131 us (0.87)
  the two profiles are of different devices: /device:TPU:4 before, /device:TPU:24 now
where the time goes in v2:
time: 131 us
  waiting for transfers between devices  45.4 us (35%)
  starting transfers between devices  43.7 us (33%)
  local copies, waits for them, and re-layouts  22.1 us (17%)
  Pallas kernels  19.1 us (15%)
    ppermute x11, waiting for transfers between devices, along_x(): return lax.ppermute(value, 'st', pairs)  33 us
    unnamed x40, local copies, waits for them, and re-layouts  17.7 us
    ppermute x11, starting transfers between devices, along_x(): return lax.ppermute(value, 'st', pairs)  16.1 us
    ppermute x11, starting transfers between devices, along_y(): return lax.ppermute(value, 'st', pairs)  15.5 us
    ppermute x8, starting transfers between devices, along_dom(): return lax.ppermute(value, 'dom', [(i, (i + by) % 16) for i in range(16)])  12.1 us
    ppermute x8, waiting for transfers between devices, along_dom(): return lax.ppermute(value, 'dom', [(i, (i + by) % 16) for i in range(16)])  7.49 us
    pallas_call x1, Pallas kernels, coef_all(): pl.pallas_call(kernel, grid=(64 // ROWS,), out_shape=[jax.ShapeDtypeStruc...  6.15 us
    ppermute x11, waiting for transfers between devices, along_y(): return lax.ppermute(value, 'st', pairs)  4.92 us
  transfers between devices with their start and end apart: 30, of which 11 were waited for; matrix products, arithmetic and copies ran while one was open for 4% of the time, Pallas kernels for 4%

profile of v2, /device:TPU:24, one launch (start us, length us, event | category | flops | bytes accessed | tf_op | source)
XLA Modules:
  0.0 130.7 jit_solution(18445662747677550639)
XLA Ops:
  2.5 5.9 %collective-permute-start = (bf16[16,32,128]{2,1,0:T(8,128)(2,1)S(1)}, bf16[16,32,128]{2,1,0:T(8,128)(2,1)S(1)}, u32[]{:S(2)}, u32[]{:S(2)}) collective-permute-start(bf16[16,32,128]{2,1,0:T(8,128)(2,1)S(1)} %get-tuple-element.37), channel_id=1, source_target_pairs={{0,224},{16,240},{32,0},{48,16},{64,32},{80,48},{96,64},{112,80},{... | collective-permute-start | bytes 393224 | tf_op jit(solution)/shard_map/ppermute | solution.py:23
  11.1 5.8 %copy-done = bf16[64,8,128,128]{3,2,1,0:T(8,128)(2,1)S(1)} copy-done((bf16[64,8,128,128]{3,2,1,0:T(8,128)(2,1)S(1)}, bf16[64,8,128,128]{3,2,1,0:T(8,128)(2,1)}, u32[]{:S(2)}) %copy-start) | copy-done | bytes 16777240
  17.9 2.8 %coef_own.1.first_ref = f32[64,32,128]{2,1,0:T(8,128)S(1)} custom-call(s32[64,8]{1,0:T(8,128)S(1)} %copy.19.ref_ref, bf16[64,8,128,128]{3,2,1,0:T(8,128)(2,1)S(1)} %copy-done, bf16[32,8192]{1,0:T(8,128)(2,1)S(1)} %copy-done.2), custom_call_target="tpu_custom_call" | custom-call | flops 134217728 | bytes 6291456 | tf_op jit(solution)/shard_map/coef_own/pallas_call | solution.py:77
  20.8 6.2 %coef_all.1 = (bf16[65,32,128]{2,1,0:T(8,128)(2,1)S(1)}, bf16[16,32,128]{2,1,0:T(8,128)(2,1)S(1)}, bf16[16,32,128]{2,1,0:T(8,128)(2,1)S(1)}, bf16[16,32,128]{2,1,0:T(8,128)(2,1)S(1)}, bf16[16,32,128]{2,1,0:T(8,128)(2,1)S(1)}) custom-call(s32[64,8]{1,0:T(8,128)S(1)} %copy.19.ref_ref, s32[1,64]{1,0:T(1,128)S(1)} %bitcast.7, s32[4,16]{1,0:T(4,128)S(1)} %bitcast.6, ...), custom_call_target="tpu_custom_call" | custom-call | flops 402653184 | bytes 14680064 | tf_op jit(solution)/shard_map/coef_all/pallas_call | solution.py:136
  27.0 2.8 %collective-permute-start.7 = (bf16[65,32,128]{2,1,0:T(8,128)(2,1)S(1)}, bf16[65,32,128]{2,1,0:T(8,128)(2,1)S(1)}, u32[]{:S(2)}, u32[]{:S(2)}) collective-permute-start(bf16[65,32,128]{2,1,0:T(8,128)(2,1)S(1)} %get-tuple-element.41.own), channel_id=1, source_target_pairs={{0,12},{1,13},{2,14},{3,15},{4,0},{5,1},{6,2},{7,3},{8,4},{9,5},{1... | collective-permute-start | bytes 1597448 | tf_op jit(solution)/shard_map/ppermute | solution.py:28
  30.6 2.5 %collective-permute-start.4 = (bf16[65,32,128]{2,1,0:T(8,128)(2,1)S(1)}, bf16[65,32,128]{2,1,0:T(8,128)(2,1)S(1)}, u32[]{:S(2)}, u32[]{:S(2)}) collective-permute-start(bf16[65,32,128]{2,1,0:T(8,128)(2,1)S(1)} %get-tuple-element.41.own), channel_id=1, source_target_pairs={{0,1},{1,2},{2,3},{3,0},{4,5},{5,6},{6,7},{7,4},{8,9},{9,10},{10,1... | collective-permute-start | bytes 1597448 | tf_op jit(solution)/shard_map/ppermute | solution.py:33
  33.1 2.5 %collective-permute-start.12 = (bf16[16,32,128]{2,1,0:T(8,128)(2,1)S(1)}, bf16[16,32,128]{2,1,0:T(8,128)(2,1)S(1)}, u32[]{:S(2)}, u32[]{:S(2)}) collective-permute-start(bf16[16,32,128]{2,1,0:T(8,128)(2,1)S(1)} %get-tuple-element.49), channel_id=1, source_target_pairs={{0,224},{16,240},{32,0},{48,16},{64,32},{80,48},{96,64},{112,80},{... | collective-permute-start | bytes 393224 | tf_op jit(solution)/shard_map/ppermute | solution.py:23
  35.6 5.8 %collective-permute-done.7.hx = bf16[65,32,128]{2,1,0:T(8,128)(2,1)S(1)} collective-permute-done((bf16[65,32,128]{2,1,0:T(8,128)(2,1)S(1)}, bf16[65,32,128]{2,1,0:T(8,128)(2,1)S(1)}, u32[]{:S(2)}, u32[]{:S(2)}) %collective-permute-start.7) | collective-permute-done | bytes 532512 | tf_op jit(solution)/shard_map/ppermute | solution.py:28
  41.5 2.3 %collective-permute-start.13 = (bf16[16,32,128]{2,1,0:T(8,128)(2,1)S(1)}, bf16[16,32,128]{2,1,0:T(8,128)(2,1)S(1)}, u32[]{:S(2)}, u32[]{:S(2)}) collective-permute-start(bf16[16,32,128]{2,1,0:T(8,128)(2,1)S(1)} %get-tuple-element.50), channel_id=1, source_target_pairs={{0,240},{16,0},{32,16},{48,32},{64,48},{80,64},{96,80},{112,96},{1... | collective-permute-start | bytes 393224 | tf_op jit(solution)/shard_map/ppermute | solution.py:23
  46.3 4.9 %collective-permute-done.14 = bf16[16,32,128]{2,1,0:T(8,128)(2,1)S(1)} collective-permute-done((bf16[16,32,128]{2,1,0:T(8,128)(2,1)S(1)}, bf16[16,32,128]{2,1,0:T(8,128)(2,1)S(1)}, u32[]{:S(2)}, u32[]{:S(2)}) %collective-permute-start.14) | collective-permute-done | bytes 131104 | tf_op jit(solution)/shard_map/ppermute | solution.py:23
  52.6 3.0 %collective-permute-start.21 = (bf16[64,32,128]{2,1,0:T(8,128)(2,1)S(1)}, bf16[64,32,128]{2,1,0:T(8,128)(2,1)S(1)}, u32[]{:S(2)}, u32[]{:S(2)}) collective-permute-start(bf16[64,32,128]{2,1,0:T(8,128)(2,1)S(1)} %constant_dynamic-update-slice_fusion.own), channel_id=1, source_target_pairs={{0,12},{1,13},{2,14},{3,15},{4,0},{5,1},{6,2},{7,3},{8,4},{9,5},{1... | collective-permute-start | bytes 1572872 | tf_op jit(solution)/shard_map/ppermute | solution.py:28
  56.0 2.8 %collective-permute-start.16 = (bf16[64,32,128]{2,1,0:T(8,128)(2,1)S(1)}, bf16[64,32,128]{2,1,0:T(8,128)(2,1)S(1)}, u32[]{:S(2)}, u32[]{:S(2)}) collective-permute-start(bf16[64,32,128]{2,1,0:T(8,128)(2,1)S(1)} %constant_dynamic-update-slice_fusion.own), channel_id=1, source_target_pairs={{0,1},{1,2},{2,3},{3,0},{4,5},{5,6},{6,7},{7,4},{8,9},{9,10},{10,1... | collective-permute-start | bytes 1572872 | tf_op jit(solution)/shard_map/ppermute | solution.py:33
  58.8 3.5 %collective-permute-start.11 = (bf16[33,32,128]{2,1,0:T(8,128)(2,1)S(1)}, bf16[33,32,128]{2,1,0:T(8,128)(2,1)S(1)}, u32[]{:S(2)}, u32[]{:S(2)}) collective-permute-start(bf16[33,32,128]{2,1,0:T(8,128)(2,1)S(1)} %slice.27), channel_id=1, source_target_pairs={{0,12},{1,13},{2,14},{3,15},{4,0},{5,1},{6,2},{7,3},{8,4},{9,5},{1... | collective-permute-start | bytes 811016 | tf_op jit(solution)/shard_map/ppermute | solution.py:28
  62.4 5.4 %collective-permute-done.21.hx = bf16[64,32,128]{2,1,0:T(8,128)(2,1)S(1)} collective-permute-done((bf16[64,32,128]{2,1,0:T(8,128)(2,1)S(1)}, bf16[64,32,128]{2,1,0:T(8,128)(2,1)S(1)}, u32[]{:S(2)}, u32[]{:S(2)}) %collective-permute-start.21) | collective-permute-done | bytes 524320 | tf_op jit(solution)/shard_map/ppermute | solution.py:28
  67.8 3.1 %collective-permute-done.20.lx = bf16[64,32,128]{2,1,0:T(8,128)(2,1)S(1)} collective-permute-done((bf16[64,32,128]{2,1,0:T(8,128)(2,1)S(1)}, bf16[64,32,128]{2,1,0:T(8,128)(2,1)S(1)}, u32[]{:S(2)}, u32[]{:S(2)}) %collective-permute-start.20) | collective-permute-done | bytes 524320 | tf_op jit(solution)/shard_map/ppermute | solution.py:28
  70.9 3.0 %collective-permute-start.8 = (bf16[32,32,128]{2,1,0:T(8,128)(2,1)S(1)}, bf16[32,32,128]{2,1,0:T(8,128)(2,1)S(1)}, u32[]{:S(2)}, u32[]{:S(2)}) collective-permute-start(bf16[32,32,128]{2,1,0:T(8,128)(2,1)S(1)} %slice.24), channel_id=1, source_target_pairs={{0,1},{1,2},{2,3},{3,0},{4,5},{5,6},{6,7},{7,4},{8,9},{9,10},{10,1... | collective-permute-start | bytes 786440 | tf_op jit(solution)/shard_map/ppermute | solution.py:33
  81.9 3.2 %collective-permute-start.18 = (bf16[32,32,128]{2,1,0:T(8,128)(2,1)}, bf16[32,32,128]{2,1,0:T(8,128)(2,1)}, u32[]{:S(2)}, u32[]{:S(2)}) collective-permute-start(bf16[32,32,128]{2,1,0:T(8,128)(2,1)} %slice.32), channel_id=1, source_target_pairs={{0,1},{1,2},{2,3},{3,0},{4,5},{5,6},{6,7},{7,4},{8,9},{9,10},{10,1... | collective-permute-start | bytes 786440 | tf_op jit(solution)/shard_map/ppermute | solution.py:33
  88.1 2.7 %density_own.1 = (bf16[64,32,128]{2,1,0:T(8,128)(2,1)S(1)}, f32[4,32,16,128]{3,2,1,0:T(8,128)S(1)}, bf16[4,32,16,128]{3,2,1,0:T(8,128)(2,1)S(1)}, bf16[4,32,16,1...) custom-call(s32[2]{0:T(128)S(1)} %pad_add_fusion.here_ref, ...), custom_call_target="tpu_custom_call" | custom-call | flops 134217728 | bytes 7340032 | tf_op jit(solution)/shard_map/density_own/pallas_call | solution.py:219
  93.9 3.7 %density_rest.1 = (f32[4,32,16,128]{3,2,1,0:T(8,128)S(1)}, bf16[4,32,16,128]{3,2,1,0:T(8,128)(2,1)S(1)}, bf16[4,32,16,128]{3,2,1,0:T(8,128)(2,1)S(1)}, bf16[4,32...) custom-call(s32[64,8]{1,0:T(8,128)S(1)} %copy.19.ref_ref, ...), custom_call_target="tpu_custom_call", output_to_operand_aliasing={{0}: (11, {}), {1}: (12, {}), {2}: (13, {}), {3}: (14, {}),... | custom-call | flops 402653184 | bytes 10485760 | tf_op jit(solution)/shard_map/density_rest/pallas_call | solution.py:257
  97.7 3.2 %collective-permute-start.25 = (bf16[4,32,16,128]{3,2,1,0:T(8,128)(2,1)S(1)}, bf16[4,32,16,128]{3,2,1,0:T(8,128)(2,1)S(1)}, u32[]{:S(2)}, u32[]{:S(2)}) collective-permute-start(bf16[4,32,16,128]{3,2,1,0:T(8,128)(2,1)S(1)} %get-tuple-element.63), channel_id=1, source_target_pairs={{0,8},{1,9},{2,10},{3,11},{4,12},{5,13},{6,14},{7,15},{8,0},{9,1},... | collective-permute-start | bytes 1572872 | tf_op jit(solution)/shard_map/ppermute | solution.py:28
  104.7 8.9 %collective-permute-done.24.refs_1_ = bf16[4,32,16,128]{3,2,1,0:T(8,128)(2,1)S(1)} collective-permute-done((bf16[4,32,16,128]{3,2,1,0:T(8,128)(2,1)S(1)}, bf16[4,32,16,128]{3,2,1,0:T(8,128)(2,1)S(1)}, u32[]{:S(2)}, u32[]{:S(2)}) %collective-permute-start.24) | collective-permute-done | bytes 524320 | tf_op jit(solution)/shard_map/ppermute | solution.py:28
  114.1 8.0 %collective-permute-done.25.refs_2_ = bf16[4,32,16,128]{3,2,1,0:T(8,128)(2,1)S(1)} collective-permute-done((bf16[4,32,16,128]{3,2,1,0:T(8,128)(2,1)S(1)}, bf16[4,32,16,128]{3,2,1,0:T(8,128)(2,1)S(1)}, u32[]{:S(2)}, u32[]{:S(2)}) %collective-permute-start.25) | collective-permute-done | bytes 524320 | tf_op jit(solution)/shard_map/ppermute | solution.py:28
  122.7 4.9 %collective-permute-done.29.refs_7_ = bf16[4,32,16,128]{3,2,1,0:T(8,128)(2,1)S(1)} collective-permute-done((bf16[4,32,16,128]{3,2,1,0:T(8,128)(2,1)S(1)}, bf16[4,32,16,128]{3,2,1,0:T(8,128)(2,1)S(1)}, u32[]{:S(2)}, u32[]{:S(2)}) %collective-permute-start.29) | collective-permute-done | bytes 524320 | tf_op jit(solution)/shard_map/ppermute | solution.py:33
  127.6 3.1 %finish.1 = f32[64,8,8,128]{3,2,1,0:T(8,128)} custom-call(s32[1,64]{1,0:T(1,128)S(1)} %bitcast.8, f32[4,32,16,128]{3,2,1,0:T(8,128)S(1)} %get-tuple-element.61.refs_0_, bf16[4,32,16,128]{3,2,1,0:T(8,128)(2,1)S(1)} %collective-permute-done.24.refs_1_, bf16[4,32,16,128]{3,2,1,0:T(8,128)(2,1)S(1)} %collective-permute-done.25.refs_2_, ...), custom_call_target="tpu_custom_call" | custom-call | bytes 7340032 | tf_op jit(solution)/shard_map/finish/pallas_call | solution.py:294
  (93 shorter events, 30.3 us)
Async XLA Ops:
  2.5 18.3 %collective-permute-start = (bf16[16,32,128]{2,1,0:T(8,128)(2,1)S(1)}, bf16[16,32,128]{2,1,0:T(8,128)(2,1)S(1)}, u32[]{:S(2)}, u32[]{:S(2)}) collective-permute-start(bf16[16,32,128]{2,1,0:T(8,128)(2,1)S(1)} %get-tuple-element.37), channel_id=1, source_target_pairs={{0,224},{16,240},{32,0},{48,16},{64,32},{80,48},{96,64},{112,80},{... | collective-permute-start | bytes 393224 | tf_op jit(solution)/shard_map/ppermute | solution.py:23
  8.4 12.4 %collective-permute-start.1 = (bf16[16,32,128]{2,1,0:T(8,128)(2,1)S(1)}, bf16[16,32,128]{2,1,0:T(8,128)(2,1)S(1)}, u32[]{:S(2)}, u32[]{:S(2)}) collective-permute-start(bf16[16,32,128]{2,1,0:T(8,128)(2,1)S(1)} %get-tuple-element.38), channel_id=1, source_target_pairs={{0,240},{16,0},{32,16},{48,32},{64,48},{80,64},{96,80},{112,96},{1... | collective-permute-start | bytes 393224 | tf_op jit(solution)/shard_map/ppermute | solution.py:23
  8.6 12.2 %collective-permute-start.2 = (bf16[16,32,128]{2,1,0:T(8,128)(2,1)S(1)}, bf16[16,32,128]{2,1,0:T(8,128)(2,1)S(1)}, u32[]{:S(2)}, u32[]{:S(2)}) collective-permute-start(bf16[16,32,128]{2,1,0:T(8,128)(2,1)S(1)} %get-tuple-element.39), channel_id=1, source_target_pairs={{0,16},{16,32},{32,48},{48,64},{64,80},{80,96},{96,112},{112,128},... | collective-permute-start | bytes 393224 | tf_op jit(solution)/shard_map/ppermute | solution.py:23
  8.9 11.9 %collective-permute-start.3 = (bf16[16,32,128]{2,1,0:T(8,128)(2,1)S(1)}, bf16[16,32,128]{2,1,0:T(8,128)(2,1)S(1)}, u32[]{:S(2)}, u32[]{:S(2)}) collective-permute-start(bf16[16,32,128]{2,1,0:T(8,128)(2,1)S(1)} %get-tuple-element.40), channel_id=1, source_target_pairs={{0,32},{16,48},{32,64},{48,80},{64,96},{80,112},{96,128},{112,144}... | collective-permute-start | bytes 393224 | tf_op jit(solution)/shard_map/ppermute | solution.py:23
  27.0 14.5 %collective-permute-start.7 = (bf16[65,32,128]{2,1,0:T(8,128)(2,1)S(1)}, bf16[65,32,128]{2,1,0:T(8,128)(2,1)S(1)}, u32[]{:S(2)}, u32[]{:S(2)}) collective-permute-start(bf16[65,32,128]{2,1,0:T(8,128)(2,1)S(1)} %get-tuple-element.41.own), channel_id=1, source_target_pairs={{0,12},{1,13},{2,14},{3,15},{4,0},{5,1},{6,2},{7,3},{8,4},{9,5},{1... | collective-permute-start | bytes 1597448 | tf_op jit(solution)/shard_map/ppermute | solution.py:28
  29.8 15.0 %collective-permute-start.6 = (bf16[65,32,128]{2,1,0:T(8,128)(2,1)S(1)}, bf16[65,32,128]{2,1,0:T(8,128)(2,1)S(1)}, u32[]{:S(2)}, u32[]{:S(2)}) collective-permute-start(bf16[65,32,128]{2,1,0:T(8,128)(2,1)S(1)} %get-tuple-element.41.own), channel_id=1, source_target_pairs={{0,4},{1,5},{2,6},{3,7},{4,8},{5,9},{6,10},{7,11},{8,12},{9,13},{1... | collective-permute-start | bytes 1597448 | tf_op jit(solution)/shard_map/ppermute | solution.py:28
  29.9 15.0 %collective-permute-start.5 = (bf16[65,32,128]{2,1,0:T(8,128)(2,1)S(1)}, bf16[65,32,128]{2,1,0:T(8,128)(2,1)S(1)}, u32[]{:S(2)}, u32[]{:S(2)}) collective-permute-start(bf16[65,32,128]{2,1,0:T(8,128)(2,1)S(1)} %get-tuple-element.41.own), channel_id=1, source_target_pairs={{0,3},{1,0},{2,1},{3,2},{4,7},{5,4},{6,5},{7,6},{8,11},{9,8},{10,9... | collective-permute-start | bytes 1597448 | tf_op jit(solution)/shard_map/ppermute | solution.py:33
  30.6 14.3 %collective-permute-start.4 = (bf16[65,32,128]{2,1,0:T(8,128)(2,1)S(1)}, bf16[65,32,128]{2,1,0:T(8,128)(2,1)S(1)}, u32[]{:S(2)}, u32[]{:S(2)}) collective-permute-start(bf16[65,32,128]{2,1,0:T(8,128)(2,1)S(1)} %get-tuple-element.41.own), channel_id=1, source_target_pairs={{0,1},{1,2},{2,3},{3,0},{4,5},{5,6},{6,7},{7,4},{8,9},{9,10},{10,1... | collective-permute-start | bytes 1597448 | tf_op jit(solution)/shard_map/ppermute | solution.py:33
  33.1 11.8 %collective-permute-start.12 = (bf16[16,32,128]{2,1,0:T(8,128)(2,1)S(1)}, bf16[16,32,128]{2,1,0:T(8,128)(2,1)S(1)}, u32[]{:S(2)}, u32[]{:S(2)}) collective-permute-start(bf16[16,32,128]{2,1,0:T(8,128)(2,1)S(1)} %get-tuple-element.49), channel_id=1, source_target_pairs={{0,224},{16,240},{32,0},{48,16},{64,32},{80,48},{96,64},{112,80},{... | collective-permute-start | bytes 393224 | tf_op jit(solution)/shard_map/ppermute | solution.py:23
  52.6 15.2 %collective-permute-start.21 = (bf16[64,32,128]{2,1,0:T(8,128)(2,1)S(1)}, bf16[64,32,128]{2,1,0:T(8,128)(2,1)S(1)}, u32[]{:S(2)}, u32[]{:S(2)}) collective-permute-start(bf16[64,32,128]{2,1,0:T(8,128)(2,1)S(1)} %constant_dynamic-update-slice_fusion.own), channel_id=1, source_target_pairs={{0,12},{1,13},{2,14},{3,15},{4,0},{5,1},{6,2},{7,3},{8,4},{9,5},{1... | collective-permute-start | bytes 1572872 | tf_op jit(solution)/shard_map/ppermute | solution.py:28
  55.6 15.4 %collective-permute-start.20 = (bf16[64,32,128]{2,1,0:T(8,128)(2,1)S(1)}, bf16[64,32,128]{2,1,0:T(8,128)(2,1)S(1)}, u32[]{:S(2)}, u32[]{:S(2)}) collective-permute-start(bf16[64,32,128]{2,1,0:T(8,128)(2,1)S(1)} %constant_dynamic-update-slice_fusion.own), channel_id=1, source_target_pairs={{0,4},{1,5},{2,6},{3,7},{4,8},{5,9},{6,10},{7,11},{8,12},{9,13},{1... | collective-permute-start | bytes 1572872 | tf_op jit(solution)/shard_map/ppermute | solution.py:28
  55.6 19.0 %collective-permute-start.17 = (bf16[64,32,128]{2,1,0:T(8,128)(2,1)S(1)}, bf16[64,32,128]{2,1,0:T(8,128)(2,1)S(1)}, u32[]{:S(2)}, u32[]{:S(2)}) collective-permute-start(bf16[64,32,128]{2,1,0:T(8,128)(2,1)S(1)} %constant_dynamic-update-slice_fusion.own), channel_id=1, source_target_pairs={{0,3},{1,0},{2,1},{3,2},{4,7},{5,4},{6,5},{7,6},{8,11},{9,8},{10,9... | collective-permute-start | bytes 1572872 | tf_op jit(solution)/shard_map/ppermute | solution.py:33
  56.0 20.8 %collective-permute-start.16 = (bf16[64,32,128]{2,1,0:T(8,128)(2,1)S(1)}, bf16[64,32,128]{2,1,0:T(8,128)(2,1)S(1)}, u32[]{:S(2)}, u32[]{:S(2)}) collective-permute-start(bf16[64,32,128]{2,1,0:T(8,128)(2,1)S(1)} %constant_dynamic-update-slice_fusion.own), channel_id=1, source_target_pairs={{0,1},{1,2},{2,3},{3,0},{4,5},{5,6},{6,7},{7,4},{8,9},{9,10},{10,1... | collective-permute-start | bytes 1572872 | tf_op jit(solution)/shard_map/ppermute | solution.py:33
  58.8 23.0 %collective-permute-start.11 = (bf16[33,32,128]{2,1,0:T(8,128)(2,1)S(1)}, bf16[33,32,128]{2,1,0:T(8,128)(2,1)S(1)}, u32[]{:S(2)}, u32[]{:S(2)}) collective-permute-start(bf16[33,32,128]{2,1,0:T(8,128)(2,1)S(1)} %slice.27), channel_id=1, source_target_pairs={{0,12},{1,13},{2,14},{3,15},{4,0},{5,1},{6,2},{7,3},{8,4},{9,5},{1... | collective-permute-start | bytes 811016 | tf_op jit(solution)/shard_map/ppermute | solution.py:28
  67.8 11.2 %collective-permute-start.10 = (bf16[32,32,128]{2,1,0:T(8,128)(2,1)S(1)}, bf16[32,32,128]{2,1,0:T(8,128)(2,1)S(1)}, u32[]{:S(2)}, u32[]{:S(2)}) collective-permute-start(bf16[32,32,128]{2,1,0:T(8,128)(2,1)S(1)} %slice.26), channel_id=1, source_target_pairs={{0,4},{1,5},{2,6},{3,7},{4,8},{5,9},{6,10},{7,11},{8,12},{9,13},{1... | collective-permute-start | bytes 786440 | tf_op jit(solution)/shard_map/ppermute | solution.py:28
  74.6 10.6 %collective-permute-start.9 = (bf16[33,32,128]{2,1,0:T(8,128)(2,1)}, bf16[33,32,128]{2,1,0:T(8,128)(2,1)}, u32[]{:S(2)}, u32[]{:S(2)}) collective-permute-start(bf16[33,32,128]{2,1,0:T(8,128)(2,1)} %slice.25), channel_id=1, source_target_pairs={{0,3},{1,0},{2,1},{3,2},{4,7},{5,4},{6,5},{7,6},{8,11},{9,8},{10,9... | collective-permute-start | bytes 811016 | tf_op jit(solution)/shard_map/ppermute | solution.py:33
  76.8 13.9 %collective-permute-start.23 = (bf16[32,32,128]{2,1,0:T(8,128)(2,1)}, bf16[32,32,128]{2,1,0:T(8,128)(2,1)}, u32[]{:S(2)}, u32[]{:S(2)}) collective-permute-start(bf16[32,32,128]{2,1,0:T(8,128)(2,1)} %slice.35), channel_id=1, source_target_pairs={{0,12},{1,13},{2,14},{3,15},{4,0},{5,1},{6,2},{7,3},{8,4},{9,5},{1... | collective-permute-start | bytes 786440 | tf_op jit(solution)/shard_map/ppermute | solution.py:28
  79.7 11.1 %collective-permute-start.22 = (bf16[32,32,128]{2,1,0:T(8,128)(2,1)}, bf16[32,32,128]{2,1,0:T(8,128)(2,1)}, u32[]{:S(2)}, u32[]{:S(2)}) collective-permute-start(bf16[32,32,128]{2,1,0:T(8,128)(2,1)} %slice.34), channel_id=1, source_target_pairs={{0,4},{1,5},{2,6},{3,7},{4,8},{5,9},{6,10},{7,11},{8,12},{9,13},{1... | collective-permute-start | bytes 786440 | tf_op jit(solution)/shard_map/ppermute | solution.py:28
  97.6 16.0 %collective-permute-start.24 = (bf16[4,32,16,128]{3,2,1,0:T(8,128)(2,1)S(1)}, bf16[4,32,16,128]{3,2,1,0:T(8,128)(2,1)S(1)}, u32[]{:S(2)}, u32[]{:S(2)}) collective-permute-start(bf16[4,32,16,128]{3,2,1,0:T(8,128)(2,1)S(1)} %get-tuple-element.62), channel_id=1, source_target_pairs={{0,4},{1,5},{2,6},{3,7},{4,8},{5,9},{6,10},{7,11},{8,12},{9,13},{1... | collective-permute-start | bytes 1572872 | tf_op jit(solution)/shard_map/ppermute | solution.py:28
  97.7 24.4 %collective-permute-start.25 = (bf16[4,32,16,128]{3,2,1,0:T(8,128)(2,1)S(1)}, bf16[4,32,16,128]{3,2,1,0:T(8,128)(2,1)S(1)}, u32[]{:S(2)}, u32[]{:S(2)}) collective-permute-start(bf16[4,32,16,128]{3,2,1,0:T(8,128)(2,1)S(1)} %get-tuple-element.63), channel_id=1, source_target_pairs={{0,8},{1,9},{2,10},{3,11},{4,12},{5,13},{6,14},{7,15},{8,0},{9,1},... | collective-permute-start | bytes 1572872 | tf_op jit(solution)/shard_map/ppermute | solution.py:28
  100.9 21.8 %collective-permute-start.26 = (bf16[4,32,16,128]{3,2,1,0:T(8,128)(2,1)S(1)}, bf16[4,32,16,128]{3,2,1,0:T(8,128)(2,1)S(1)}, u32[]{:S(2)}, u32[]{:S(2)}) collective-permute-start(bf16[4,32,16,128]{3,2,1,0:T(8,128)(2,1)S(1)} %get-tuple-element.64), channel_id=1, source_target_pairs={{0,12},{1,13},{2,14},{3,15},{4,0},{5,1},{6,2},{7,3},{8,4},{9,5},{1... | collective-permute-start | bytes 1572872 | tf_op jit(solution)/shard_map/ppermute | solution.py:28
  102.4 20.4 %collective-permute-start.27 = (bf16[4,32,16,128]{3,2,1,0:T(8,128)(2,1)S(1)}, bf16[4,32,16,128]{3,2,1,0:T(8,128)(2,1)S(1)}, u32[]{:S(2)}, u32[]{:S(2)}) collective-permute-start(bf16[4,32,16,128]{3,2,1,0:T(8,128)(2,1)S(1)} %get-tuple-element.66), channel_id=1, source_target_pairs={{0,1},{1,2},{2,3},{3,0},{4,5},{5,6},{6,7},{7,4},{8,9},{9,10},{10,1... | collective-permute-start | bytes 1572872 | tf_op jit(solution)/shard_map/ppermute | solution.py:33
  104.5 18.2 %collective-permute-start.28 = (bf16[4,32,16,128]{3,2,1,0:T(8,128)(2,1)S(1)}, bf16[4,32,16,128]{3,2,1,0:T(8,128)(2,1)S(1)}, u32[]{:S(2)}, u32[]{:S(2)}) collective-permute-start(bf16[4,32,16,128]{3,2,1,0:T(8,128)(2,1)S(1)} %get-tuple-element.67), channel_id=1, source_target_pairs={{0,2},{1,3},{2,0},{3,1},{4,6},{5,7},{6,4},{7,5},{8,10},{9,11},{10,... | collective-permute-start | bytes 1572872 | tf_op jit(solution)/shard_map/ppermute | solution.py:33
  113.7 13.9 %collective-permute-start.29 = (bf16[4,32,16,128]{3,2,1,0:T(8,128)(2,1)S(1)}, bf16[4,32,16,128]{3,2,1,0:T(8,128)(2,1)S(1)}, u32[]{:S(2)}, u32[]{:S(2)}) collective-permute-start(bf16[4,32,16,128]{3,2,1,0:T(8,128)(2,1)S(1)} %get-tuple-element.68), channel_id=1, source_target_pairs={{0,3},{1,0},{2,1},{3,2},{4,7},{5,4},{6,5},{7,6},{8,11},{9,8},{10,9... | collective-permute-start | bytes 1572872 | tf_op jit(solution)/shard_map/ppermute | solution.py:33
  (24 other events, 182.8 us)
